TPU v7x, 32 devices: a whole 2x2x4 slice. The times are simulated.
32 devices in a mesh: groups: 2 (over y), dp: 4 (over z), expert: 2 (over x), pair: 2 (over core).
Axes of the slice: x: 2, y: 2, z: 4, core: 2. Of those that a mesh axis runs over, the one named last changes fastest.
Arguments:
- states: bfloat16 [2, 256, 6144], P(None, ('groups', 'dp'), ('expert', 'pair')), parts along dimension 1, may hold values from -6 to 6
- base_gate_up_projection: bfloat16 [2, 256, 2, 2, 16384], P(None, ('groups', 'dp'), None, None, ('expert', 'pair')), parts along dimension 1, may hold values from -6 to 6
- route_panel_index: int32 [2, 256, 2], P(None, ('groups', 'dp')), parts along dimension 1, may hold values from 0 to 63, as said below
- adapter_down_maps: bfloat16 [64, 2, 16, 6144], P('dp', None, None, ('expert', 'pair')), may hold values from -0.078125 to 0.078125
- adapter_up_maps: bfloat16 [64, 2, 16, 16384], P('dp', None, None, ('expert', 'pair')), may hold values from -0.75 to 0.75
- magnitude_over_norm: bfloat16 [64, 2, 16384], P('dp', None, ('expert', 'pair')), may hold values from 0.5 to 2
Outputs:
- hidden_units: bfloat16 [2, 256, 2, 16384], P(None, ('groups', 'dp'), None, ('expert', 'pair')), parts along dimension 1
There are 2 independent parts, one for each index of `groups`. A program takes and returns all parts, laid end to end along the dimension named above; an argument that names none is the same for every part. Nothing has to cross between parts.
Inputs may be any that keep to these rules, and one draw needn't show every extreme that they name: `route_panel_index`: A panel u is held by owner u // 16. In each step the 64 routes of the rows of one index of dp name panels of any one owner at most 40 times, and some owner exactly 40 times.
All inputs are finite; a program needn't handle non-finite values.
Results may differ from a plain program's by a relative error of at most 0.0048.
Values may be sent and summed in bfloat16 or wider, within the bound.
No kernel may reach another device: no remote copies, remote signals or barrier semaphores. Data moves between devices by JAX's collectives and lax.ppermute only.
A program may use at most 128 MiB of HBM per device.

v0:
```python
import functools

import jax
import jax.numpy as jnp
from jax import lax
from jax.experimental import pallas as pl
from jax.experimental.pallas import tpu as pltpu
from jax.sharding import PartitionSpec as P

LANES = 128
ROW_TILE = 16
VMEM_LIMIT = 10 * 1024 * 1024
RELAY_VMEM_LIMIT = 24 * 1024 * 1024


def nt_dot(a, b):
    return lax.dot_general(a, b, (((1,), (1,)), ((), ())), preferred_element_type=jnp.float32)


def earlier_in_step(steps, rows):
    routes = 2 * steps * rows
    first = lax.broadcasted_iota(jnp.int32, (routes, routes), 0)
    second = lax.broadcasted_iota(jnp.int32, (routes, routes), 1)
    same = (first // rows) % steps == (second // rows) % steps
    return jnp.where(same & (first < second), 1.0, 0.0).astype(jnp.bfloat16)


def low_kernel(count, steps, rows, cap, slots, me_ref, down_ref, *refs):
    state_refs, (part_ref, info_ref) = refs[:count], refs[count:]
    panels, _, rank, width = down_ref.shape
    routes = 2 * steps * rows
    me = me_ref[0].astype(jnp.float32)
    down = down_ref[...].reshape(panels * 2 * rank, width)
    pick = jnp.where(
        lax.broadcasted_iota(jnp.int32, (8, LANES), 0) == lax.broadcasted_iota(jnp.int32, (8, LANES), 1), 1.0, 0.0
    ).astype(jnp.bfloat16)
    before = earlier_in_step(steps, rows)
    lane = lax.broadcasted_iota(jnp.int32, (1, routes), 1)
    step_of = ((lane // rows) % steps).astype(jnp.float32)
    panel_of = (lax.broadcasted_iota(jnp.int32, (panels * 2 * rank, routes), 0) // (2 * rank)).astype(jnp.float32)
    for s in range(count):
        one = state_refs[s][...]
        both = jnp.concatenate([one, one], axis=0)
        numbers = nt_dot(pick, both[:, width:])
        owner = jnp.where(lane < routes // 2, numbers[0:1], numbers[1:2])
        within = jnp.where(lane < routes // 2, numbers[2:3], numbers[3:4])
        mine = owner == me
        rank_of = jnp.dot(
            jnp.broadcast_to(jnp.where(mine, 1.0, 0.0), (8, routes)).astype(jnp.bfloat16),
            before,
            preferred_element_type=jnp.float32,
        )[0:1]
        slot = jnp.where(mine, step_of * cap + rank_of, -1.0)
        held = jnp.where(mine, within, -1.0)
        cols = pl.ds(s * routes, routes)
        info_ref[:, cols] = jnp.concatenate([slot, held, jnp.zeros((6, routes), jnp.float32)], axis=0)
        low = nt_dot(down, both[:, :width])
        low = jnp.where(panel_of == held, low, 0.0)
        part_ref[:, cols] = jnp.sum(low.reshape(panels, 2 * rank, routes), axis=0)


def delta_kernel(count, slots, info_ref, low_ref, up_ref, *refs):
    out_refs, (lhs_ref,) = refs[:count], refs[count:]
    panels, rank, tile = up_ref.shape
    routes = info_ref.shape[1] // count

    @pl.when((pl.program_id(0) == 0) & (pl.program_id(1) == 0))
    def _():
        low = low_ref[...].astype(jnp.bfloat16).astype(jnp.float32)
        panel_of = (lax.broadcasted_iota(jnp.int32, (panels * rank, routes), 0) // rank).astype(jnp.float32)
        slot_of = lax.broadcasted_iota(jnp.int32, (slots, routes), 0).astype(jnp.float32)
        for s in range(count):
            cols = slice(s * routes, (s + 1) * routes)
            slot, held = info_ref[0:1, cols], info_ref[1:2, cols]
            place = jnp.where(slot_of == slot, 1.0, 0.0).astype(jnp.bfloat16)
            for p in range(2):
                wide = jnp.concatenate([low[p * rank : (p + 1) * rank, cols]] * panels, axis=0)
                wide = jnp.where(panel_of == held, wide, 0.0).astype(jnp.bfloat16)
                lhs_ref[p, s * slots : (s + 1) * slots, :] = nt_dot(place, wide).astype(jnp.bfloat16)

    p = pl.program_id(0)
    up = up_ref[...].reshape(panels * rank, tile)
    delta = jnp.dot(lhs_ref[p], up, preferred_element_type=jnp.float32).astype(jnp.bfloat16)
    for s in range(count):
        out_refs[s][...] = delta[s * slots : (s + 1) * slots]


def gate_kernel(count, group_ref, pick_ref, panel_ref, base_ref, mine_ref, other_ref, *refs):
    blocks, out_ref = refs[: 2 * count], refs[2 * count]
    slots = blocks[0].shape[0]
    group = group_ref[0]
    adapted = []
    for p in range(2):
        delta = None
        for s in range(count):
            part = jnp.dot(
                pick_ref[:, s * slots : (s + 1) * slots],
                blocks[p * count + s][...],
                preferred_element_type=jnp.float32,
            )
            delta = part if delta is None else delta + part
        scales = jnp.where(group == p, mine_ref[...], other_ref[...])
        scale = jnp.dot(panel_ref[...], scales, preferred_element_type=jnp.float32)
        adapted.append(scale * (base_ref[p].astype(jnp.float32) + delta))
    gate, value = adapted
    out_ref[...] = (gate / (1.0 + jnp.exp(-gate)) * value).astype(out_ref.dtype)


CHUNK = 24
LAG = 2
GAP = LAG * CHUNK
ROW_STEP = 8
MAGNITUDE_ROWS = 16
QUEUE_ROWS = (144, 168, 192, 216)


def chunk_rows(total):
    return [(at, min(CHUNK, total - at)) for at in range(0, total, CHUNK)]


def right_layout(n):
    gap = float(GAP)
    zero = jnp.zeros_like(n[0][0])
    place = {}

    def put(link, j, d, first, split=None, second=None):
        place[link, j, d] = (first, split, second)

    put(0, 0, 3, zero)
    put(0, 0, 2, n[0][3])
    put(0, 0, 1, n[0][3] + n[0][2])
    end = n[0][3] + n[0][2] + n[0][1]
    early = jnp.maximum(jnp.minimum(n[1][2], gap - n[1][3]), 0.0)
    far = jnp.maximum(n[1][3], gap)
    late = far + n[0][3] + n[1][2] - early
    put(1, 1, 3, zero)
    put(1, 0, 3, far)
    put(1, 1, 2, n[1][3], early, far + n[0][3] - early)
    put(1, 0, 2, late)
    end = jnp.maximum(end, late + n[0][2])
    one = jnp.maximum(n[2][3] + float(MAGNITUDE_ROWS), gap)
    two = jnp.maximum(one + n[1][3], far + gap)
    put(2, 2, 3, zero, zero + float(GAP - MAGNITUDE_ROWS), zero + float(MAGNITUDE_ROWS))
    put(2, 1, 3, one)
    put(2, 0, 3, two)
    return place, jnp.maximum(end, two + n[0][3])


def relay_plan_kernel(steps, rows, panels, me_ref, part_ref, *refs):
    count = 4
    route_refs, outs = refs[:3], refs[3:]
    info_ref, longest_ref, forward_ref, first_ref, held_ref, arrive_ref, panel_ref = outs
    routes = 2 * steps * rows
    limit = forward_ref.shape[1]
    me = me_ref[0]
    before = jnp.where(
        lax.broadcasted_iota(jnp.int32, (routes, routes), 0) < lax.broadcasted_iota(jnp.int32, (routes, routes), 1),
        1.0,
        0.0,
    ).astype(jnp.bfloat16)
    owners = lax.broadcasted_iota(jnp.int32, (8, routes), 0).astype(jnp.float32)
    same = lax.broadcasted_iota(jnp.int32, (routes, routes), 0) == lax.broadcasted_iota(jnp.int32, (routes, routes), 1)
    same = jnp.where(same, 1.0, 0.0).astype(jnp.bfloat16)
    owner, order, tally = [], [], []
    info_ref[...] = jnp.full(info_ref.shape, -1.0, jnp.float32)
    came = [ref[...].astype(jnp.float32) for ref in route_refs]
    came = came[:2] + [came[2][: came[0].shape[0]], came[2][came[0].shape[0] :]]
    for s in range(count):
        numbers = sum(jnp.where((part_ref[0] ^ i) == s, came[i], 0.0) for i in range(count))
        owner.append(numbers[0:1])
        hits = jnp.where(owners == owner[s], 1.0, 0.0)
        ahead = jnp.dot(hits.astype(jnp.bfloat16), before, preferred_element_type=jnp.float32)
        order.append(jnp.sum(ahead * hits, axis=0, keepdims=True))
        tally.append(jnp.sum(hits, axis=1, keepdims=True))
        cols = slice(s * routes, (s + 1) * routes)
        info_ref[0:1, cols] = jnp.where(owner[s] == me.astype(jnp.float32), numbers[1:2], -1.0)
        if s == 0:
            within = numbers[1:2]

    def position(place, link, d, s, turned, owners_from, owners_to):
        found = jnp.full((1, routes), -1.0, jnp.float32)
        for j in range(owners_from, owners_to):
            first, split, second = place[link, j, d]
            at = first + order[s]
            if split is not None:
                at = jnp.where(order[s] < split, at, second + order[s])
            found = jnp.where(owner[s] == float(3 - j if turned else j), at, found)
        return found

    for case in range(count):

        @pl.when(me == case)
        def _():
            longest = None
            for turned in (False, True):
                node = 3 - case if turned else case
                n = [[None] * count for _ in range(count)]
                for j in range(count):
                    for d in range(count):
                        s = (case - d) % count
                        if turned:
                            n[3 - j][3 - d] = tally[s][j : j + 1]
                        else:
                            n[j][d] = tally[s][j : j + 1]
                place, end = right_layout(n)
                longest = end if longest is None else jnp.maximum(longest, end)
                row = 1 if turned == (case % 2 == 1) else 4
                for d in range(node + 1, count):
                    s = (case - (3 - d if turned else d)) % count
                    cols = slice(s * routes, (s + 1) * routes)
                    info_ref[row : row + 1, cols] = position(place, node, d, s, turned, node, node + 1)
                    if node > 0:
                        info_ref[row + 1 : row + 2, cols] = position(place, node, d, s, turned, 0, node)
                        info_ref[row + 2 : row + 3, cols] = position(place, node - 1, d, s, turned, 0, node)
                if node > 0:
                    arrive = 7 if turned == (case % 2 == 0) else 8
                    info_ref[arrive : arrive + 1, 0:routes] = position(place, node - 1, node, 0, turned, 0, node)
            longest_ref[...] = jnp.broadcast_to(longest, longest_ref.shape)
            blocks = [j ^ case for j in range(count)]
            if case in (0, count - 1):
                blocks = [block ^ 1 if block >= 2 else block for block in blocks]
            block_of = sum(jnp.where(owner[0] == float(j), float(blocks[j]), 0.0) for j in range(count))
            stands = block_of * panels + within
            depth = count * panels
            rows_of = lax.broadcasted_iota(jnp.int32, (depth, routes), 0).astype(jnp.float32)
            panel_ref[...] = nt_dot(same, jnp.where(rows_of == stands, 1.0, 0.0).astype(jnp.bfloat16)).astype(
                jnp.bfloat16
            )

    shape = forward_ref.shape[1:]
    same_half = lax.broadcasted_iota(jnp.int32, shape, 0) % 2 == lax.broadcasted_iota(jnp.int32, shape, 1) % 2
    for way in range(2):
        passed = nt_dot(placed(info_ref, 3 * way + 2, shape[0]), placed(info_ref, 3 * way + 3, shape[0]))
        forward_ref[way] = jnp.where(same_half, passed, 0.0).astype(jnp.bfloat16)
        for i in range(LAG):
            rows = pl.ds(2 * CHUNK * (2 * i + way), 2 * CHUNK)
            first_ref[rows, :] = placed(info_ref, 3 * way + 1, 2 * CHUNK, i * CHUNK)
        stands = placed(info_ref, 7 + way, shape[0])[:, :routes]
        stands = nt_dot(same, stands)
        for p in range(2):
            half = lax.broadcasted_iota(jnp.int32, stands.shape, 1) % 2 == p
            arrive_ref[way, p * routes : (p + 1) * routes, :] = jnp.where(half, stands, 0.0).astype(jnp.bfloat16)
    panel = jnp.broadcast_to(info_ref[0:1, :], (8, info_ref.shape[1])).astype(jnp.bfloat16)
    panel = nt_dot(first_ref[...], panel)[:, 0:1]
    half_row = lax.broadcasted_iota(jnp.int32, held_ref.shape, 0)
    lane = lax.broadcasted_iota(jnp.int32, held_ref.shape, 1)
    both = held_ref.shape[1] // panels
    here = ((lane % both) // (both // 2) == half_row % 2) & ((lane // both).astype(jnp.float32) == panel)
    held_ref[...] = jnp.where(here, 1.0, 0.0).astype(jnp.bfloat16)


def relay_load_kernel(down_ref, up_ref, down_out, up_out, sems):
    copies = [
        pltpu.make_async_copy(down_ref, down_out, sems.at[0]),
        pltpu.make_async_copy(up_ref, up_out, sems.at[1]),
    ]
    for copy in copies:
        copy.start()
    for copy in copies:
        copy.wait()


def relay_branch_kernel(totals, own_ref, other_ref, out_ref):
    longest = jnp.max(jnp.maximum(own_ref[...], other_ref[...]))
    out_ref[0] = sum((longest > float(total)).astype(jnp.int32) for total in totals[:-1])


def relay_low_kernel(info_ref, down_ref, half_ref, beside_ref, *refs):
    state_refs, (part_ref, join_ref) = refs[:-2], refs[-2:]
    panels, _, rank, width = down_ref.shape
    routes = info_ref.shape[1] // len(state_refs)
    down = down_ref[...].reshape(panels * 2 * rank, width)
    panel_of = (lax.broadcasted_iota(jnp.int32, (panels * 2 * rank, routes), 0) // (2 * rank)).astype(jnp.float32)
    join_ref[:panels, :] = beside_ref[...]
    join_ref[panels:, :] = half_ref[...]
    for s, state_ref in enumerate(state_refs):
        one = state_ref[...]
        cols = slice(s * routes, (s + 1) * routes)
        low = nt_dot(down, jnp.concatenate([one, one], axis=0))
        low = jnp.where(panel_of == info_ref[0:1, cols], low, 0.0)
        part_ref[:, cols] = jnp.sum(low.reshape(panels, 2 * rank, routes), axis=0)


def summed_low(own_ref, core_ref, far_ref, diag_ref):
    low = (own_ref[...] + core_ref[...]) + (far_ref[...] + diag_ref[...])
    return low.astype(jnp.bfloat16).astype(jnp.float32)


def spread_low(low, info_ref, panels):
    held = info_ref[0:1, :]
    panel_of = lax.broadcasted_iota(jnp.int32, (panels * low.shape[0], held.shape[1]), 0) // low.shape[0]
    wide = jnp.concatenate([low] * panels, axis=0)
    return jnp.where(panel_of.astype(jnp.float32) == held, wide, 0.0).astype(jnp.bfloat16)


def placed(info_ref, row, half_rows, start=0):
    at = info_ref[row : row + 1, :] - float(start)
    slot_of = lax.broadcasted_iota(jnp.int32, (half_rows, at.shape[1]), 0) // 2
    return jnp.where(slot_of.astype(jnp.float32) == at, 1.0, 0.0).astype(jnp.bfloat16)


def low_rows(place, wide, panels, half_of):
    rows = nt_dot(place, wide)
    both = rows.shape[1] // panels
    own_half = half_of == (lax.broadcasted_iota(jnp.int32, rows.shape, 1) % both) // (both // 2)
    return jnp.where(own_half, rows, 0.0).astype(jnp.bfloat16)


def column_tiles(hidden, body, most=512):
    tile = min(most, hidden)

    @pl.loop(0, hidden // tile)
    def _(i):
        body(pl.ds(pl.multiple_of(i * tile, tile), tile))


def relay_first_kernel(
    index, first_ref, held_ref, own_ref, core_ref, far_ref, diag_ref, up_ref, *refs
):
    across_refs, (outer_ref, middle_ref, lhs_ref) = refs[:-3], refs[-3:]
    low = summed_low(own_ref, core_ref, far_ref, diag_ref).astype(jnp.bfloat16)
    here = slice(4 * CHUNK * index, 4 * CHUNK * (index + 1))
    rows = nt_dot(first_ref[here, :], low).astype(jnp.bfloat16)
    shape = (low.shape[0], held_ref.shape[1])
    source = lax.broadcasted_iota(jnp.int32, shape, 1) % shape[0]
    spread = jnp.where(lax.broadcasted_iota(jnp.int32, shape, 0) == source, 1.0, 0.0).astype(jnp.bfloat16)
    wide = jnp.dot(rows, spread, preferred_element_type=jnp.float32).astype(jnp.bfloat16)
    lhs_ref[...] = wide * held_ref[here, :]

    def body(cols):
        delta = jnp.dot(lhs_ref[...], up_ref[:, cols], preferred_element_type=jnp.float32).astype(jnp.bfloat16)
        outer_ref[:, cols] = delta[: 2 * CHUNK]
        middle_ref[:, cols] = delta[2 * CHUNK :]
        for across_ref in across_refs:
            at = 2 * CHUNK - across_ref.shape[0]
            outer_ref[at:, cols] = delta[at : 2 * CHUNK] + across_ref[:, cols]

    column_tiles(up_ref.shape[1], body, 1024)


def relay_rows_kernel(panels, info_ref, own_ref, core_ref, far_ref, diag_ref, lhs_ref, local_ref):
    wide = spread_low(summed_low(own_ref, core_ref, far_ref, diag_ref), info_ref, panels)
    for way in range(2):
        half_of = lax.broadcasted_iota(jnp.int32, lhs_ref.shape[1:], 0) % 2
        lhs_ref[way] = low_rows(placed(info_ref, 3 * way + 1, lhs_ref.shape[1]), wide, panels, half_of)
    routes = local_ref.shape[0] // 2
    shape = (2 * routes, routes)
    same = lax.broadcasted_iota(jnp.int32, shape, 0) % routes == lax.broadcasted_iota(jnp.int32, shape, 1)
    half_of = lax.broadcasted_iota(jnp.int32, local_ref.shape, 0) // routes
    local_ref[...] = low_rows(jnp.where(same, 1.0, 0.0).astype(jnp.bfloat16), wide[:, :routes], panels, half_of)


def relay_stack_kernel(me_ref, half_ref, beside_ref, across_ref, second_ref, out_ref):
    depth = half_ref.shape[0]
    out_ref[:depth] = half_ref[...]
    out_ref[depth : 2 * depth] = beside_ref[...]
    end = (me_ref[0] == 0) | (me_ref[0] == 3)

    @pl.when(end)
    def _():
        out_ref[2 * depth :] = second_ref[second_ref.shape[0] - 2 * depth :]

    @pl.when(jnp.logical_not(end))
    def _():
        out_ref[2 * depth :] = across_ref[...]


def relay_chunk_kernel(first, count, known, lhs_ref, forward_ref, up_ref, *refs):
    came, out_refs = refs[:-2], refs[-2:]
    here = slice(2 * first, 2 * (first + count))

    def body(cols):
        lhs = jnp.concatenate([lhs_ref[0, here, :], lhs_ref[1, here, :]], axis=0)
        delta = jnp.dot(lhs, up_ref[:, cols], preferred_element_type=jnp.float32)
        for way in range(2):
            blocks = came[len(came) // 2 :] if way == 0 else came[: len(came) // 2]
            rows = jnp.concatenate([block[:, cols] for block in blocks], axis=0)
            passed = jnp.dot(forward_ref[way, here, : 2 * known], rows, preferred_element_type=jnp.float32)
            out_refs[way][:, cols] = (delta[2 * way * count : 2 * (way + 1) * count] + passed).astype(jnp.bfloat16)

    column_tiles(up_ref.shape[1], body)


def relay_pick_kernel(known, arrive_ref, local_ref, up_ref, *refs):
    came, out_ref = refs[:-1], refs[-1]
    routes = out_ref.shape[1]

    def body(cols):
        delta = jnp.dot(local_ref[...], up_ref[:, cols], preferred_element_type=jnp.float32)
        delta = delta.astype(jnp.bfloat16).astype(jnp.float32)
        for way in range(2):
            blocks = came[way * len(came) // 2 : (way + 1) * len(came) // 2]
            rows = jnp.concatenate([block[:, cols] for block in blocks], axis=0)
            delta += jnp.dot(arrive_ref[way, :, : 2 * known], rows, preferred_element_type=jnp.float32)
        for p in range(2):
            out_ref[p, :, cols] = delta[p * routes : (p + 1) * routes].astype(out_ref.dtype)

    column_tiles(up_ref.shape[1], body)


def relay_gate_kernel(
    known, group_ref, arrive_ref, panel_ref, mine_ref, other_ref, base_ref, early_ref, outer_ref, middle_ref, out_ref, pick_ref
):
    rows = out_ref.shape[0]
    routes = 2 * rows
    size = outer_ref.shape[0]
    group = group_ref[0]
    shape = (size, arrive_ref.shape[2])
    last = lax.broadcasted_iota(jnp.int32, shape, 1) == 2 * known + lax.broadcasted_iota(jnp.int32, shape, 0)
    last = jnp.where(last, 1.0, 0.0).astype(jnp.bfloat16)
    for way in range(2):
        pick_ref[:, way * size : (way + 1) * size] = nt_dot(arrive_ref[way], last).astype(jnp.bfloat16)

    def body(cols):
        scales = [
            jnp.dot(panel_ref[...], ref[:, cols], preferred_element_type=jnp.float32) for ref in (mine_ref, other_ref)
        ]
        late = jnp.concatenate([outer_ref[:, cols], middle_ref[:, cols]], axis=0)
        picked = jnp.dot(pick_ref[...], late, preferred_element_type=jnp.float32)
        adapted = []
        for p in range(2):
            delta = early_ref[p, :, cols].astype(jnp.float32) + picked[p * routes : (p + 1) * routes]
            scale = jnp.where(group == p, scales[0], scales[1])
            adapted.append(scale * (base_ref[p, :, cols].astype(jnp.float32) + delta))
        gate, value = adapted
        hidden = (gate / (1.0 + jnp.exp(-gate)) * value).astype(out_ref.dtype)
        for k in range(2):
            out_ref[:, k, cols] = hidden[k * rows : (k + 1) * rows]

    column_tiles(out_ref.shape[2], body)


def relay_base_kernel(base_ref, out_ref):
    rows = base_ref.shape[0]

    def body(cols):
        for k in range(2):
            for p in range(2):
                out_ref[p, k * rows : (k + 1) * rows, cols] = base_ref[:, k, p, cols]

    column_tiles(base_ref.shape[3], body)


def relayed(seen, numbers, which, magnitude, base, down, up):
    count = 4
    me, group = lax.axis_index("dp"), lax.axis_index("groups")
    steps, rows, hidden = base.shape[0], base.shape[1], base.shape[-1]
    panels, _, rank, _ = down.shape
    routes = 2 * steps * rows
    cap = max(2, (5 * rows + count - 1) // count)
    limit = max(
        3 * steps * cap,
        2 * routes,
        GAP + 2 * steps * cap,
        GAP + routes,
        2 * GAP + steps * cap,
    )
    limit = -(-limit // ROW_STEP) * ROW_STEP
    bf16, f32, i32 = jnp.bfloat16, jnp.float32, jnp.int32
    vmem = pl.BlockSpec(memory_space=pltpu.VMEM)
    smem = pl.BlockSpec(memory_space=pltpu.SMEM)

    def kernel(body, inputs, outputs, scalars=0, specs=None, out_specs=None, scratch=(), cost=1):
        return pl.pallas_call(
            body,
            out_shape=[jax.ShapeDtypeStruct(shape, dtype) for shape, dtype in outputs],
            in_specs=specs or [smem] * scalars + [vmem] * (len(inputs) - scalars),
            out_specs=out_specs or [vmem] * len(outputs),
            scratch_shapes=list(scratch),
            compiler_params=pltpu.CompilerParams(vmem_limit_bytes=RELAY_VMEM_LIMIT),
            cost_estimate=pl.CostEstimate(flops=0, bytes_accessed=cost << 20, transcendentals=0),
        )(*inputs)

    base = base.reshape(steps * rows, 2, 2, hidden)
    outer_pairs, middle_pair = [(0, 1), (1, 0), (2, 3), (3, 2)], [(1, 2), (2, 1)]
    half = lax.dynamic_index_in_dim(magnitude, group, axis=1, keepdims=False)
    beside = lax.ppermute(half, "dp", outer_pairs)
    half, *numbers = lax.optimization_barrier((half, *numbers))
    info, longest, forward, first, held, arrive, panel = kernel(
        functools.partial(relay_plan_kernel, steps, rows, panels),
        [me.reshape(1).astype(i32), which.reshape(1).astype(i32), *numbers],
        [
            ((16, count * routes), f32),
            ((8, LANES), f32),
            ((2, 2 * limit, 2 * limit), bf16),
            ((4 * GAP, count * routes), bf16),
            ((4 * GAP, 2 * panels * rank), bf16),
            ((2, 2 * routes, 2 * limit), bf16),
            ((routes, count * panels), bf16),
        ],
        scalars=2,
        cost=128,
    )
    down, up, longest = lax.optimization_barrier((down, up, longest))
    down, up_rows = kernel(
        relay_load_kernel,
        [down, up.reshape(panels * 2 * rank, hidden)],
        [(down.shape, bf16), ((panels * 2 * rank, hidden), bf16)],
        specs=[pl.BlockSpec(memory_space=pltpu.HBM)] * 2,
        scratch=[pltpu.SemaphoreType.DMA((2,))],
    )
    totals = [total for total in QUEUE_ROWS if total < limit] + [limit]
    [branch] = kernel(
        functools.partial(relay_branch_kernel, totals),
        [longest, lax.ppermute(longest, "groups", [(0, 1), (1, 0)])],
        [((1,), i32)],
        out_specs=[smem],
    )

    down, up_rows, branch, *seen = lax.optimization_barrier((down, up_rows, branch, *seen))
    part, join = kernel(
        relay_low_kernel,
        [info, down, half, beside, *seen],
        [((2 * rank, count * routes), f32), ((2 * panels, hidden), bf16)],
    )
    lows = [part]
    for mask in (1, 2, 3):
        lows.append(lax.ppermute(part, ("expert", "pair"), [(i, i ^ mask) for i in range(4)]))
    across = lax.ppermute(join, "dp", middle_pair)

    def early(index, first, held, lows, up_rows, *across):
        return kernel(
            functools.partial(relay_first_kernel, index),
            [first, held, *lows, up_rows, *across],
            [((2 * CHUNK, hidden), bf16)] * 2,
            scratch=[pltpu.VMEM((4 * CHUNK, 2 * panels * rank), bf16)],
        )

    outer_first, middle_first = early(0, first, held, lows, up_rows)

    def flow(total, operands):
        (outer_first, middle_first, first, held, info, lows, forward, up_rows) = operands[:8]
        arrive, panel, base, half, beside, across = operands[8:]
        chunks = chunk_rows(total)
        got_outer, got_middle = [], []
        for k, (start, size) in enumerate(chunks):
            if k == 0:
                outer, middle = outer_first, middle_first
            elif k < LAG:
                outer, middle = early(k, first, held, lows, up_rows, across)
            else:
                if k == LAG:
                    info, base, *lows = lax.optimization_barrier((info, base, *lows, outer))[:-1]
                    [base_rows] = kernel(relay_base_kernel, [base], [((2, routes, hidden), bf16)])
                    base_rows, info = lax.optimization_barrier((base_rows, info))
                    lhs, local = kernel(
                        functools.partial(relay_rows_kernel, panels),
                        [info, *lows],
                        [((2, 2 * limit, 2 * panels * rank), bf16), ((2 * routes, 2 * panels * rank), bf16)],
                    )
                known = k + 1 - LAG
                outer, middle = kernel(
                    functools.partial(relay_chunk_kernel, start, size, chunks[known][0]),
                    [lhs, forward, up_rows, *got_outer[:known], *got_middle[:known]],
                    [((2 * size, hidden), bf16)] * 2,
                    cost=4 + k,
                )
            got_middle.append(lax.ppermute(middle, "dp", middle_pair))
            got_outer.append(lax.ppermute(outer, "dp", outer_pairs))
        [mine] = kernel(
            relay_stack_kernel,
            [me.reshape(1).astype(i32), half, beside, across, got_outer[1]],
            [((count * panels, hidden), bf16)],
            scalars=1,
        )
        other = lax.ppermute(mine, "groups", [(0, 1), (1, 0)])
        last, size = chunks[-1]
        [picked] = kernel(
            functools.partial(relay_pick_kernel, last),
            [arrive, local, up_rows, *got_outer[:-1], *got_middle[:-1]],
            [((2, routes, hidden), bf16)],
        )
        picked, *final = lax.optimization_barrier((picked, got_outer[-1], got_middle[-1]))
        [out] = kernel(
            functools.partial(relay_gate_kernel, last),
            [group.reshape(1).astype(i32), arrive, panel, mine, other, base_rows, picked, *final],
            [((steps * rows, 2, hidden), bf16)],
            scalars=1,
            scratch=[pltpu.VMEM((2 * routes, 4 * size), bf16)],
        )
        return out

    operands = (
        outer_first, middle_first, first, held, info, lows, forward, up_rows,
        arrive, panel, base, half, beside, across,
    )
    out = lax.switch(branch[0], [functools.partial(flow, total) for total in totals], operands)
    return out.reshape(steps, rows, 2, hidden)


def on_device(states, base, route_panels, down, up, magnitude):
    count = lax.axis_size("dp")
    me = lax.axis_index("dp")
    group = lax.axis_index("groups")
    steps, rows, width = states.shape
    hidden = base.shape[-1]
    panels, _, rank, _ = down.shape
    routes = 2 * steps * rows
    cap = max(2, (5 * rows + count - 1) // count)
    slots = -(-steps * cap // ROW_TILE) * ROW_TILE
    bf16, f32, i32 = jnp.bfloat16, jnp.float32, jnp.int32

    def turn(x, shift):
        return lax.ppermute(x, "dp", [(i, (i + shift) % count) for i in range(count)])

    if (count, lax.axis_size("expert"), lax.axis_size("pair")) == (4, 2, 2):
        one = states.reshape(steps * rows, width)
        flat = route_panels.transpose(2, 0, 1).reshape(1, routes)
        number = jnp.concatenate([flat // panels, flat % panels], axis=0).astype(bf16)
        number = jnp.pad(number, ((0, ROW_TILE - 2), (0, 0)))
        which = 2 * lax.axis_index("expert") + lax.axis_index("pair")
        one, number = lax.optimization_barrier((one, number))
        far = [(4 * d + e, 4 * ((d + e) % count) + e) for d in range(count) for e in range(4)]
        near = lax.ppermute(number, ("dp", "expert", "pair"), far)
        beside = lax.ppermute(near, "pair", [(0, 1), (1, 0)])
        both = lax.ppermute(jnp.concatenate([near, beside], axis=0), "expert", [(0, 1), (1, 0)])
        one, near = lax.optimization_barrier((one, near))
        seen = [one] + [turn(one, s) for s in range(1, count)]
        return relayed(seen, [near, beside, both], which, magnitude, base, down, up)

    pairs = route_panels.reshape(steps * rows, 2)
    numbers = jnp.concatenate([pairs // panels, pairs % panels], axis=1).astype(bf16)
    sent = jnp.concatenate(
        [states.reshape(steps * rows, width), jnp.pad(numbers, ((0, 0), (0, LANES - 4)))], axis=1
    )
    seen = [sent] + [turn(sent, s) for s in range(1, count)]

    half = lax.dynamic_index_in_dim(magnitude, group, axis=1, keepdims=False)
    mine = jnp.concatenate([half] + [turn(half, s) for s in range(1, count)], axis=0)
    other = lax.ppermute(mine, "groups", [(0, 1), (1, 0)])

    vmem = pl.BlockSpec(memory_space=pltpu.VMEM)
    smem = pl.BlockSpec(memory_space=pltpu.SMEM)
    params = pltpu.CompilerParams(vmem_limit_bytes=VMEM_LIMIT)
    part, info = pl.pallas_call(
        functools.partial(low_kernel, count, steps, rows, cap, slots),
        out_shape=(
            jax.ShapeDtypeStruct((2 * rank, count * routes), f32),
            jax.ShapeDtypeStruct((8, count * routes), f32),
        ),
        in_specs=[smem] + [vmem] * (1 + count),
        out_specs=(vmem, vmem),
        compiler_params=params,
    )(me.reshape(1).astype(i32), down, *seen)

    low = lax.psum(part, ("expert", "pair"))

    tile = min(1024, hidden)
    col_tiles = hidden // tile
    whole = lambda shape: pl.BlockSpec(shape, lambda p, n: (0,) * len(shape))
    deltas = pl.pallas_call(
        functools.partial(delta_kernel, count, slots),
        out_shape=[jax.ShapeDtypeStruct((slots, 2 * hidden), bf16)] * count,
        grid=(2, col_tiles),
        in_specs=[whole(info.shape)]
        + [whole(low.shape)]
        + [pl.BlockSpec((panels, None, rank, tile), lambda p, n: (0, p, 0, n))],
        out_specs=[pl.BlockSpec((slots, tile), lambda p, n: (0, p * col_tiles + n))] * count,
        scratch_shapes=[pltpu.VMEM((2, count * slots, panels * rank), bf16)],
        compiler_params=params,
    )(info, low, up)
    got = [deltas[0]] + [turn(deltas[s], count - s) for s in range(1, count)]

    ordered = route_panels.transpose(2, 0, 1).reshape(2, steps, rows)
    owner, within = ordered // panels, ordered % panels
    by_step = owner.transpose(1, 0, 2).reshape(steps, 2 * rows)
    earlier = jnp.tril(jnp.ones((2 * rows, 2 * rows), jnp.bool_), -1)
    rank_of = jnp.sum((by_step[:, :, None] == by_step[:, None, :]) & earlier[None], axis=2, dtype=i32)
    slot = rank_of + jnp.arange(steps, dtype=i32)[:, None] * cap
    slot = slot.reshape(steps, 2, rows).transpose(1, 0, 2).reshape(routes)
    owner, within = owner.reshape(routes), within.reshape(routes)
    ahead = (owner - me) % count
    behind = (me - owner) % count
    pick = (jnp.arange(count * slots, dtype=i32)[None, :] == (ahead * slots + slot)[:, None]).astype(bf16)
    panel = (jnp.arange(count * panels, dtype=i32)[None, :] == (behind * panels + within)[:, None]).astype(bf16)
    base_rows = base.transpose(3, 2, 0, 1, 4).reshape(2, routes, hidden)

    tile = min(512, hidden)
    col_tiles = hidden // tile
    whole = lambda shape: pl.BlockSpec(shape, lambda n: (0,) * len(shape))
    col = lambda depth, p: pl.BlockSpec((depth, tile), lambda n, p=p: (0, p * col_tiles + n))
    out = pl.pallas_call(
        functools.partial(gate_kernel, count),
        out_shape=jax.ShapeDtypeStruct((routes, hidden), bf16),
        grid=(col_tiles,),
        in_specs=[smem, whole(pick.shape), whole(panel.shape)]
        + [pl.BlockSpec((2, routes, tile), lambda n: (0, 0, n))]
        + [col(count * panels, 0)] * 2
        + [col(slots, 0)] * count
        + [col(slots, 1)] * count,
        out_specs=col(routes, 0),
        compiler_params=params,
    )(group.reshape(1).astype(i32), pick, panel, base_rows, mine, other, *got, *got)
    return out.reshape(2, steps, rows, hidden).transpose(1, 2, 0, 3)


def solution(mesh):
    return jax.shard_map(
        on_device,
        mesh=mesh,
        in_specs=(
            P(None, ("groups", "dp"), ("expert", "pair")),
            P(None, ("groups", "dp"), None, None, ("expert", "pair")),
            P(None, ("groups", "dp"), None),
            P("dp", None, None, ("expert", "pair")),
            P("dp", None, None, ("expert", "pair")),
            P("dp", None, ("expert", "pair")),
        ),
        out_specs=P(None, ("groups", "dp"), None, ("expert", "pair")),
        check_vma=False,
    )
```

profile of v0, /device:TPU:0, one launch (start us, length us, event | category | flops | bytes accessed | tf_op | source)
XLA Modules:
  0.0 108.0 jit_solution(68183024364784344)
XLA Ops:
  0.0 0.7 copy.14
  1.5 3.1 %collective-permute-start.91 = (bf16[64,1536]{1,0:T(8,128)(2,1)}, bf16[64,1536]{1,0:T(8,128)(2,1)S(1)}, u32[]{:S(2)}, u32[]{:S(2)}) collective-permute-start(bf16[64,1536]{1,0:T(8,128)(2,1)} %bitcast.26), channel_id=1, source_target_pairs={{0,4},{4,8},{8,12},{12,0},{1,5},{5,9},{9,13},{13,1},{2,6},{6,10},{... | collective-permute-start | bytes 589832 | tf_op jit(solution)/shard_map/ppermute | solution.py:604
  4.6 2.6 %collective-permute-start.92 = (bf16[64,1536]{1,0:T(8,128)(2,1)}, bf16[64,1536]{1,0:T(8,128)(2,1)S(1)}, u32[]{:S(2)}, u32[]{:S(2)}) collective-permute-start(bf16[64,1536]{1,0:T(8,128)(2,1)} %bitcast.27), channel_id=1, source_target_pairs={{0,8},{4,12},{8,0},{12,4},{1,9},{5,13},{9,1},{13,5},{2,10},{6,14},... | collective-permute-start | bytes 589832 | tf_op jit(solution)/shard_map/ppermute | solution.py:604
  7.2 1.3 %collective-permute-start.93 = (bf16[64,1536]{1,0:T(8,128)(2,1)}, bf16[64,1536]{1,0:T(8,128)(2,1)S(1)}, u32[]{:S(2)}, u32[]{:S(2)}) collective-permute-start(bf16[64,1536]{1,0:T(8,128)(2,1)} %bitcast.28), channel_id=1, source_target_pairs={{0,12},{4,0},{8,4},{12,8},{1,13},{5,1},{9,5},{13,9},{2,14},{6,2},{... | collective-permute-start | bytes 589832 | tf_op jit(solution)/shard_map/ppermute | solution.py:604
  9.0 0.7 collective-permute-start.94
  9.8 3.0 %collective-permute-start.88 = (bf16[16,128]{1,0:T(8,128)(2,1)S(1)}, bf16[16,128]{1,0:T(8,128)(2,1)S(1)}, u32[]{:S(2)}, u32[]{:S(2)}) collective-permute-start(bf16[16,128]{1,0:T(8,128)(2,1)S(1)} %collective-permute-done.87.refs_0_), channel_id=1, source_target_pairs={{0,1},{1,0},{2,3},{3,2},{4,5},{5,4},{6,7},{7,6},{8,9},{9,8},{10,11... | collective-permute-start | bytes 12296 | tf_op jit(solution)/shard_map/ppermute | solution.py:615
  12.8 0.8 collective-permute-done.88.refs_1_
  13.6 4.5 %collective-permute-start.89 = (bf16[32,128]{1,0:T(8,128)(2,1)S(1)}, bf16[32,128]{1,0:T(8,128)(2,1)S(1)}, u32[]{:S(2)}, u32[]{:S(2)}) collective-permute-start(bf16[32,128]{1,0:T(8,128)(2,1)S(1)} %pad_maximum_fusion), channel_id=1, source_target_pairs={{0,2},{2,0},{1,3},{3,1},{4,6},{6,4},{5,7},{7,5},{8,10},{10,8},{9,1... | collective-permute-start | bytes 24584 | tf_op jit(solution)/shard_map/ppermute | solution.py:616
  18.1 1.6 %collective-permute-done.89.refs_2_ = bf16[32,128]{1,0:T(8,128)(2,1)S(1)} collective-permute-done((bf16[32,128]{1,0:T(8,128)(2,1)S(1)}, bf16[32,128]{1,0:T(8,128)(2,1)S(1)}, u32[]{:S(2)}, u32[]{:S(2)}) %collective-permute-start.89) | collective-permute-done | bytes 8224 | tf_op jit(solution)/shard_map/ppermute | solution.py:616
  19.7 1.3 %shard_map.69 = (f32[16,512]{1,0:T(8,128)S(1)}, f32[8,128]{1,0:T(8,128)S(1)}, bf16[2,512,512]{2,1,0:T(8,128)(2,1)S(1)}, bf16[192,512]{1,0:T(8,128)(2,1)S(1)}, bf...) custom-call(s32[1]{0:T(128)} %bitcast.15.me_ref, s32[1]{0:T(128)} %bitcast.16.part_ref, ...), custom_call_target="tpu_custom_call" | custom-call | bytes 134217728 | tf_op jit(solution)/shard_map/pallas_call | solution.py:464
  21.0 1.6 %collective-permute-start.90 = (f32[8,128]{1,0:T(8,128)S(1)}, f32[8,128]{1,0:T(8,128)S(1)}, u32[]{:S(2)}, u32[]{:S(2)}) collective-permute-start(f32[8,128]{1,0:T(8,128)S(1)} %get-tuple-element.476.own_ref), channel_id=1, source_target_pairs={{0,16},{16,0},{1,17},{17,1},{2,18},{18,2},{3,19},{19,3},{4,20},{20... | collective-permute-start | bytes 12296 | tf_op jit(solution)/shard_map/ppermute | solution.py:505
  22.6 2.2 %copy-done.2 = bf16[16,2,16,4096]{3,2,1,0:T(8,128)(2,1)S(1)} copy-done((bf16[16,2,16,4096]{3,2,1,0:T(8,128)(2,1)S(1)}, bf16[16,2,16,4096]{3,2,1,0:T(8,128)(2,1)}, u32[]{:S(2)}) %copy-start.2) | copy-done | bytes 4194328
  24.8 1.4 %copy-done.3 = bf16[16,2,16,1536]{3,2,1,0:T(8,128)(2,1)S(1)} copy-done((bf16[16,2,16,1536]{3,2,1,0:T(8,128)(2,1)S(1)}, bf16[16,2,16,1536]{3,2,1,0:T(8,128)(2,1)}, u32[]{:S(2)}) %copy-start.3) | copy-done | bytes 1572888
  27.3 1.8 %shard_map.72 = (f32[32,512]{1,0:T(8,128)S(1)}, bf16[32,4096]{1,0:T(8,128)(2,1)S(1)}) custom-call(f32[16,512]{1,0:T(8,128)S(1)} %get-tuple-element.481.info_ref, bf16[16,2,16,1536]{3,2,1,0:T(8,128)(2,1)S(1)} %get-tuple-element.482.down_ref, bf16[16,4096]{1,0:T(8,128)(2,1)S(1)} %bitcast.36, bf16[16,4096]{1,0:T(8,128)(2,1)S(1)} %collective-permute-done.94.beside_ref, ...), custom_call_target="tpu_custom_call" | custom-call | bytes 1048576 | tf_op jit(solution)/shard_map/pallas_call | solution.py:464
  29.1 0.7 collective-permute-start.98
  29.9 2.6 %collective-permute-start.96 = (f32[32,512]{1,0:T(8,128)S(1)}, f32[32,512]{1,0:T(8,128)S(1)}, u32[]{:S(2)}, u32[]{:S(2)}) collective-permute-start(f32[32,512]{1,0:T(8,128)S(1)} %get-tuple-element.488.own_ref), channel_id=1, source_target_pairs={{0,2},{1,3},{2,0},{3,1},{4,6},{5,7},{6,4},{7,5},{8,10},{9,11},{10,... | collective-permute-start | bytes 196616 | tf_op jit(solution)/shard_map/ppermute | solution.py:518
  33.3 1.9 %collective-permute-done.96.far_ref = f32[32,512]{1,0:T(8,128)S(1)} collective-permute-done((f32[32,512]{1,0:T(8,128)S(1)}, f32[32,512]{1,0:T(8,128)S(1)}, u32[]{:S(2)}, u32[]{:S(2)}) %collective-permute-start.96) | collective-permute-done | bytes 65568 | tf_op jit(solution)/shard_map/ppermute | solution.py:518
  35.2 1.4 %collective-permute-done.97.diag_ref = f32[32,512]{1,0:T(8,128)S(1)} collective-permute-done((f32[32,512]{1,0:T(8,128)S(1)}, f32[32,512]{1,0:T(8,128)S(1)}, u32[]{:S(2)}, u32[]{:S(2)}) %collective-permute-start.97) | collective-permute-done | bytes 65568 | tf_op jit(solution)/shard_map/ppermute | solution.py:518
  36.6 1.6 %shard_map.73 = (bf16[48,4096]{1,0:T(8,128)(2,1)S(1)}, bf16[48,4096]{1,0:T(8,128)(2,1)S(1)}) custom-call(bf16[192,512]{1,0:T(8,128)(2,1)S(1)} %get-tuple-element.479.first_ref, bf16[192,512]{1,0:T(8,128)(2,1)S(1)} %get-tuple-element.480.held_ref, f32[32,512]{1,0:T(8,128)S(1)} %get-tuple-element.488.own_ref, f32[32,512]{1,0:T(8,128)S(1)} %collective-permute-done.95.core_ref, ...), custom_call_target="tpu_custom_call" | custom-call | bytes 1048576 | tf_op jit(solution)/shard_map/pallas_call | solution.py:464
  38.2 67.9 %conditional.1 = (bf16[2,32,2,4096]{3,2,1,0:T(2,128)(2,1)S(1)}) conditional(s32[]{:T(128)} %bitcast.21, (s32[]{:T(128)}, s32[]{:T(128)}, bf16[192,512]{1,0:T(8,128)(2,1)S(1)}, bf16[192,512]{1,0:T(8,128)(2,1)S(1)}, f32[32,512]{1,0:T(8,128)S(1)}, /*index=5*/f32[32,512]{1,0:T(8,128)S(1)}, f32[32,512]{1,0:T(8,128)S(1)}, ...), branch_computations={%region_0.1_spmd, %region_1.2_spmd, %region_2.3_spmd, %region_3.4_... | conditional | bytes 136315808 | solution.py:587
  38.2 3.3 %collective-permute-start.15 = (bf16[48,4096]{1,0:T(8,128)(2,1)S(1)}, bf16[48,4096]{1,0:T(8,128)(2,1)S(1)}, u32[]{:S(2)}, u32[]{:S(2)}) collective-permute-start(bf16[48,4096]{1,0:T(8,128)(2,1)S(1)} %get-tuple-element.270), channel_id=1, source_target_pairs={{0,4},{4,0},{8,12},{12,8},{1,5},{5,1},{9,13},{13,9},{2,6},{6,2},{1... | collective-permute-start | bytes 1179656 | tf_op jit(solution)/shard_map/cond/branch_1_fun/ppermute | solution.py:559
  42.2 1.6 %branch_1_fun.11 = (bf16[48,4096]{1,0:T(8,128)(2,1)S(1)}, bf16[48,4096]{1,0:T(8,128)(2,1)S(1)}) custom-call(bf16[192,512]{1,0:T(8,128)(2,1)S(1)} %get-tuple-element.251.first_ref, bf16[192,512]{1,0:T(8,128)(2,1)S(1)} %get-tuple-element.252.held_ref, f32[32,512]{1,0:T(8,128)S(1)} %get-tuple-element.265.own_ref, f32[32,512]{1,0:T(8,128)S(1)} %get-tuple-element.266.core_ref, ...), custom_call_target="tpu_custom_call" | custom-call | bytes 1048576 | tf_op jit(solution)/shard_map/cond/branch_1_fun/pallas_call | solution.py:464
  43.8 3.3 %collective-permute-start.13 = (bf16[48,4096]{1,0:T(8,128)(2,1)S(1)}, bf16[48,4096]{1,0:T(8,128)(2,1)S(1)}, u32[]{:S(2)}, u32[]{:S(2)}) collective-permute-start(bf16[48,4096]{1,0:T(8,128)(2,1)S(1)} %get-tuple-element.258), channel_id=1, source_target_pairs={{0,4},{4,0},{8,12},{12,8},{1,5},{5,1},{9,13},{13,9},{2,6},{6,2},{1... | collective-permute-start | bytes 1179656 | tf_op jit(solution)/shard_map/cond/branch_1_fun/ppermute | solution.py:559
  47.8 4.5 %branch_1_fun.13.base_ref = bf16[2,128,4096]{2,1,0:T(8,128)(2,1)S(1)} custom-call(bf16[64,2,2,4096]{3,2,1,0:T(2,128)(2,1)S(1)} %get-tuple-element.261.base_ref), custom_call_target="tpu_custom_call" | custom-call | bytes 1048576 | tf_op jit(solution)/shard_map/cond/branch_1_fun/pallas_call | solution.py:464
  52.3 0.8 branch_1_fun.14
  53.1 2.0 %branch_1_fun.15 = (bf16[48,4096]{1,0:T(8,128)(2,1)S(1)}, bf16[48,4096]{1,0:T(8,128)(2,1)S(1)}) custom-call(bf16[2,512,512]{2,1,0:T(8,128)(2,1)S(1)} %get-tuple-element.271.lhs_ref, bf16[2,512,512]{2,1,0:T(8,128)(2,1)S(1)} %get-tuple-element.272.forward_ref, bf16[512,4096]{1,0:T(8,128)(2,1)S(1)} %get-tuple-element.257.up_ref, ...), custom_call_target="tpu_custom_call" | custom-call | bytes 6291456 | tf_op jit(solution)/shard_map/cond/branch_1_fun/pallas_call | solution.py:464
  55.1 2.3 %collective-permute-start.17 = (bf16[48,4096]{1,0:T(8,128)(2,1)S(1)}, bf16[48,4096]{1,0:T(8,128)(2,1)S(1)}, u32[]{:S(2)}, u32[]{:S(2)}) collective-permute-start(bf16[48,4096]{1,0:T(8,128)(2,1)S(1)} %get-tuple-element.274), channel_id=1, source_target_pairs={{0,4},{4,0},{8,12},{12,8},{1,5},{5,1},{9,13},{13,9},{2,6},{6,2},{1... | collective-permute-start | bytes 1179656 | tf_op jit(solution)/shard_map/cond/branch_1_fun/ppermute | solution.py:559
  57.4 0.7 collective-permute-start.20
  58.1 1.7 %collective-permute-done.13.second_ref.refs_1_ = bf16[48,4096]{1,0:T(8,128)(2,1)S(1)} collective-permute-done((bf16[48,4096]{1,0:T(8,128)(2,1)S(1)}, bf16[48,4096]{1,0:T(8,128)(2,1)S(1)}, u32[]{:S(2)}, u32[]{:S(2)}) %collective-permute-start.13) | collective-permute-done | bytes 393248 | tf_op jit(solution)/shard_map/cond/branch_1_fun/ppermute | solution.py:559
  59.8 2.0 %branch_1_fun.16 = (bf16[48,4096]{1,0:T(8,128)(2,1)S(1)}, bf16[48,4096]{1,0:T(8,128)(2,1)S(1)}) custom-call(bf16[2,512,512]{2,1,0:T(8,128)(2,1)S(1)} %get-tuple-element.271.lhs_ref, bf16[2,512,512]{2,1,0:T(8,128)(2,1)S(1)} %get-tuple-element.272.forward_ref, bf16[512,4096]{1,0:T(8,128)(2,1)S(1)} %get-tuple-element.257.up_ref, ...), custom_call_target="tpu_custom_call" | custom-call | bytes 7340032 | tf_op jit(solution)/shard_map/cond/branch_1_fun/pallas_call | solution.py:464
  61.9 4.0 %collective-permute-start.19 = (bf16[48,4096]{1,0:T(8,128)(2,1)S(1)}, bf16[48,4096]{1,0:T(8,128)(2,1)S(1)}, u32[]{:S(2)}, u32[]{:S(2)}) collective-permute-start(bf16[48,4096]{1,0:T(8,128)(2,1)S(1)} %get-tuple-element.276), channel_id=1, source_target_pairs={{0,4},{4,0},{8,12},{12,8},{1,5},{5,1},{9,13},{13,9},{2,6},{6,2},{1... | collective-permute-start | bytes 1179656 | tf_op jit(solution)/shard_map/cond/branch_1_fun/ppermute | solution.py:559
  65.8 0.7 collective-permute-start.22
  66.5 1.7 %collective-permute-done.17.refs_2_ = bf16[48,4096]{1,0:T(8,128)(2,1)S(1)} collective-permute-done((bf16[48,4096]{1,0:T(8,128)(2,1)S(1)}, bf16[48,4096]{1,0:T(8,128)(2,1)S(1)}, u32[]{:S(2)}, u32[]{:S(2)}) %collective-permute-start.17) | collective-permute-done | bytes 393248 | tf_op jit(solution)/shard_map/cond/branch_1_fun/ppermute | solution.py:559
  68.3 2.1 %branch_1_fun.17 = (bf16[48,4096]{1,0:T(8,128)(2,1)S(1)}, bf16[48,4096]{1,0:T(8,128)(2,1)S(1)}) custom-call(bf16[2,512,512]{2,1,0:T(8,128)(2,1)S(1)} %get-tuple-element.271.lhs_ref, bf16[2,512,512]{2,1,0:T(8,128)(2,1)S(1)} %get-tuple-element.272.forward_ref, bf16[512,4096]{1,0:T(8,128)(2,1)S(1)} %get-tuple-element.257.up_ref, ...), custom_call_target="tpu_custom_call" | custom-call | bytes 8388608 | tf_op jit(solution)/shard_map/cond/branch_1_fun/pallas_call | solution.py:464
  70.3 4.0 %collective-permute-start.21 = (bf16[48,4096]{1,0:T(8,128)(2,1)S(1)}, bf16[48,4096]{1,0:T(8,128)(2,1)S(1)}, u32[]{:S(2)}, u32[]{:S(2)}) collective-permute-start(bf16[48,4096]{1,0:T(8,128)(2,1)S(1)} %get-tuple-element.278), channel_id=1, source_target_pairs={{0,4},{4,0},{8,12},{12,8},{1,5},{5,1},{9,13},{13,9},{2,6},{6,2},{1... | collective-permute-start | bytes 1179656 | tf_op jit(solution)/shard_map/cond/branch_1_fun/ppermute | solution.py:559
  74.3 0.7 collective-permute-start.24
  75.1 1.6 %collective-permute-start.14 = (bf16[64,4096]{1,0:T(8,128)(2,1)S(1)}, bf16[64,4096]{1,0:T(8,128)(2,1)S(1)}, u32[]{:S(2)}, u32[]{:S(2)}) collective-permute-start(bf16[64,4096]{1,0:T(8,128)(2,1)S(1)} %branch_1_fun.12.mine_ref), channel_id=1, source_target_pairs={{0,16},{16,0},{1,17},{17,1},{2,18},{18,2},{3,19},{19,3},{4,20},{20... | collective-permute-start | bytes 1572872 | tf_op jit(solution)/shard_map/cond/branch_1_fun/ppermute | solution.py:566
  76.7 2.1 %branch_1_fun.18 = (bf16[48,4096]{1,0:T(8,128)(2,1)S(1)}, bf16[48,4096]{1,0:T(8,128)(2,1)S(1)}) custom-call(bf16[2,512,512]{2,1,0:T(8,128)(2,1)S(1)} %get-tuple-element.271.lhs_ref, bf16[2,512,512]{2,1,0:T(8,128)(2,1)S(1)} %get-tuple-element.272.forward_ref, bf16[512,4096]{1,0:T(8,128)(2,1)S(1)} %get-tuple-element.257.up_ref, ...), custom_call_target="tpu_custom_call" | custom-call | bytes 9437184 | tf_op jit(solution)/shard_map/cond/branch_1_fun/pallas_call | solution.py:464
  78.9 4.0 %collective-permute-start.23 = (bf16[48,4096]{1,0:T(8,128)(2,1)S(1)}, bf16[48,4096]{1,0:T(8,128)(2,1)S(1)}, u32[]{:S(2)}, u32[]{:S(2)}) collective-permute-start(bf16[48,4096]{1,0:T(8,128)(2,1)S(1)} %get-tuple-element.280), channel_id=1, source_target_pairs={{0,4},{4,0},{8,12},{12,8},{1,5},{5,1},{9,13},{13,9},{2,6},{6,2},{1... | collective-permute-start | bytes 1179656 | tf_op jit(solution)/shard_map/cond/branch_1_fun/ppermute | solution.py:559
  83.5 1.6 %collective-permute-done.21.refs_4_ = bf16[48,4096]{1,0:T(8,128)(2,1)S(1)} collective-permute-done((bf16[48,4096]{1,0:T(8,128)(2,1)S(1)}, bf16[48,4096]{1,0:T(8,128)(2,1)S(1)}, u32[]{:S(2)}, u32[]{:S(2)}) %collective-permute-start.21) | collective-permute-done | bytes 393248 | tf_op jit(solution)/shard_map/cond/branch_1_fun/ppermute | solution.py:559
  85.1 2.3 %branch_1_fun.20 = (bf16[48,4096]{1,0:T(8,128)(2,1)S(1)}, bf16[48,4096]{1,0:T(8,128)(2,1)S(1)}) custom-call(bf16[2,512,512]{2,1,0:T(8,128)(2,1)S(1)} %get-tuple-element.271.lhs_ref, bf16[2,512,512]{2,1,0:T(8,128)(2,1)S(1)} %get-tuple-element.272.forward_ref, bf16[512,4096]{1,0:T(8,128)(2,1)S(1)} %get-tuple-element.257.up_ref, ...), custom_call_target="tpu_custom_call" | custom-call | bytes 10485760 | tf_op jit(solution)/shard_map/cond/branch_1_fun/pallas_call | solution.py:464
  87.4 4.0 %collective-permute-start.26 = (bf16[48,4096]{1,0:T(8,128)(2,1)S(1)}, bf16[48,4096]{1,0:T(8,128)(2,1)S(1)}, u32[]{:S(2)}, u32[]{:S(2)}) collective-permute-start(bf16[48,4096]{1,0:T(8,128)(2,1)S(1)} %get-tuple-element.283), channel_id=1, source_target_pairs={{0,4},{4,0},{8,12},{12,8},{1,5},{5,1},{9,13},{13,9},{2,6},{6,2},{1... | collective-permute-start | bytes 1179656 | tf_op jit(solution)/shard_map/cond/branch_1_fun/ppermute | solution.py:559
  92.1 1.5 %collective-permute-done.23.refs_5_ = bf16[48,4096]{1,0:T(8,128)(2,1)S(1)} collective-permute-done((bf16[48,4096]{1,0:T(8,128)(2,1)S(1)}, bf16[48,4096]{1,0:T(8,128)(2,1)S(1)}, u32[]{:S(2)}, u32[]{:S(2)}) %collective-permute-start.23) | collective-permute-done | bytes 393248 | tf_op jit(solution)/shard_map/cond/branch_1_fun/ppermute | solution.py:559
  93.5 4.7 %branch_1_fun.19.early_ref = bf16[2,128,4096]{2,1,0:T(8,128)(2,1)S(1)} custom-call(bf16[2,256,512]{2,1,0:T(8,128)(2,1)S(1)} %get-tuple-element.245.arrive_ref, bf16[256,512]{1,0:T(8,128)(2,1)S(1)} %get-tuple-element.269.local_ref, bf16[512,4096]{1,0:T(8,128)(2,1)S(1)} %get-tuple-element.257.up_ref, bf16[48,4096]{1,0:T(8,128)(2,1)S(1)} %collective-permute-done.15.refs_0_, ...), custom_call_target="tpu_custom_call" | custom-call | bytes 1048576 | tf_op jit(solution)/shard_map/cond/branch_1_fun/pallas_call | solution.py:464
  98.2 3.3 %collective-permute-done.26.outer_ref = bf16[48,4096]{1,0:T(8,128)(2,1)S(1)} collective-permute-done((bf16[48,4096]{1,0:T(8,128)(2,1)S(1)}, bf16[48,4096]{1,0:T(8,128)(2,1)S(1)}, u32[]{:S(2)}, u32[]{:S(2)}) %collective-permute-start.26) | collective-permute-done | bytes 393248 | tf_op jit(solution)/shard_map/cond/branch_1_fun/ppermute | solution.py:559
  101.5 4.1 %branch_1_fun.21 = bf16[64,2,4096]{2,1,0:T(2,128)(2,1)S(1)} custom-call(s32[1]{0:T(128)} %bitcast.3.group_ref, bf16[2,256,512]{2,1,0:T(8,128)(2,1)S(1)} %get-tuple-element.245.arrive_ref, bf16[128,64]{1,0:T(8,128)(2,1)S(1)} %get-tuple-element.246.panel_ref, bf16[64,4096]{1,0:T(8,128)(2,1)S(1)} %branch_1_fun.12.mine_ref, ...), custom_call_target="tpu_custom_call" | custom-call | bytes 1048576 | tf_op jit(solution)/shard_map/cond/branch_1_fun/pallas_call | solution.py:464
  106.1 1.0 copy-done.6
  107.0 0.9 copy-done.1
  (44 shorter events, 5.3 us)
Async XLA Ops:
  0.0 8.6 %copy-start = (bf16[16,2,4096]{2,1,0:T(2,128)(2,1)S(1)}, bf16[16,2,4096]{2,1,0:T(2,128)(2,1)}, u32[]{:S(2)}) copy-start(bf16[16,2,4096]{2,1,0:T(2,128)(2,1)} %param.16) | copy-start | bytes 786436
  0.8 0.7 collective-permute-start.87
  1.5 25.7 %collective-permute-start.91 = (bf16[64,1536]{1,0:T(8,128)(2,1)}, bf16[64,1536]{1,0:T(8,128)(2,1)S(1)}, u32[]{:S(2)}, u32[]{:S(2)}) collective-permute-start(bf16[64,1536]{1,0:T(8,128)(2,1)} %bitcast.26), channel_id=1, source_target_pairs={{0,4},{4,8},{8,12},{12,0},{1,5},{5,9},{9,13},{13,1},{2,6},{6,10},{... | collective-permute-start | bytes 589832 | tf_op jit(solution)/shard_map/ppermute | solution.py:604
  4.6 22.7 %collective-permute-start.92 = (bf16[64,1536]{1,0:T(8,128)(2,1)}, bf16[64,1536]{1,0:T(8,128)(2,1)S(1)}, u32[]{:S(2)}, u32[]{:S(2)}) collective-permute-start(bf16[64,1536]{1,0:T(8,128)(2,1)} %bitcast.27), channel_id=1, source_target_pairs={{0,8},{4,12},{8,0},{12,4},{1,9},{5,13},{9,1},{13,5},{2,10},{6,14},... | collective-permute-start | bytes 589832 | tf_op jit(solution)/shard_map/ppermute | solution.py:604
  7.2 20.1 %collective-permute-start.93 = (bf16[64,1536]{1,0:T(8,128)(2,1)}, bf16[64,1536]{1,0:T(8,128)(2,1)S(1)}, u32[]{:S(2)}, u32[]{:S(2)}) collective-permute-start(bf16[64,1536]{1,0:T(8,128)(2,1)} %bitcast.28), channel_id=1, source_target_pairs={{0,12},{4,0},{8,4},{12,8},{1,13},{5,1},{9,5},{13,9},{2,14},{6,2},{... | collective-permute-start | bytes 589832 | tf_op jit(solution)/shard_map/ppermute | solution.py:604
  9.0 18.3 %collective-permute-start.94 = (bf16[16,4096]{1,0:T(8,128)(2,1)S(1)}, bf16[16,4096]{1,0:T(8,128)(2,1)S(1)}, u32[]{:S(2)}, u32[]{:S(2)}) collective-permute-start(bf16[16,4096]{1,0:T(8,128)(2,1)S(1)} %bitcast.35), channel_id=1, source_target_pairs={{0,4},{4,0},{8,12},{12,8},{1,5},{5,1},{9,13},{13,9},{2,6},{6,2},{1... | collective-permute-start | bytes 393224 | tf_op jit(solution)/shard_map/ppermute | solution.py:477
  9.8 3.8 %collective-permute-start.88 = (bf16[16,128]{1,0:T(8,128)(2,1)S(1)}, bf16[16,128]{1,0:T(8,128)(2,1)S(1)}, u32[]{:S(2)}, u32[]{:S(2)}) collective-permute-start(bf16[16,128]{1,0:T(8,128)(2,1)S(1)} %collective-permute-done.87.refs_0_), channel_id=1, source_target_pairs={{0,1},{1,0},{2,3},{3,2},{4,5},{5,4},{6,7},{7,6},{8,9},{9,8},{10,11... | collective-permute-start | bytes 12296 | tf_op jit(solution)/shard_map/ppermute | solution.py:615
  13.6 6.1 %collective-permute-start.89 = (bf16[32,128]{1,0:T(8,128)(2,1)S(1)}, bf16[32,128]{1,0:T(8,128)(2,1)S(1)}, u32[]{:S(2)}, u32[]{:S(2)}) collective-permute-start(bf16[32,128]{1,0:T(8,128)(2,1)S(1)} %pad_maximum_fusion), channel_id=1, source_target_pairs={{0,2},{2,0},{1,3},{3,1},{4,6},{6,4},{5,7},{7,5},{8,10},{10,8},{9,1... | collective-permute-start | bytes 24584 | tf_op jit(solution)/shard_map/ppermute | solution.py:616
  21.0 5.6 %collective-permute-start.90 = (f32[8,128]{1,0:T(8,128)S(1)}, f32[8,128]{1,0:T(8,128)S(1)}, u32[]{:S(2)}, u32[]{:S(2)}) collective-permute-start(f32[8,128]{1,0:T(8,128)S(1)} %get-tuple-element.476.own_ref), channel_id=1, source_target_pairs={{0,16},{16,0},{1,17},{17,1},{2,18},{18,2},{3,19},{19,3},{4,20},{20... | collective-permute-start | bytes 12296 | tf_op jit(solution)/shard_map/ppermute | solution.py:505
  22.6 2.2 %copy-start.2 = (bf16[16,2,16,4096]{3,2,1,0:T(8,128)(2,1)S(1)}, bf16[16,2,16,4096]{3,2,1,0:T(8,128)(2,1)}, u32[]{:S(2)}) copy-start(bf16[16,2,16,4096]{3,2,1,0:T(8,128)(2,1)} %param.15) | copy-start | bytes 12582916
  24.8 1.4 %copy-start.3 = (bf16[16,2,16,1536]{3,2,1,0:T(8,128)(2,1)S(1)}, bf16[16,2,16,1536]{3,2,1,0:T(8,128)(2,1)}, u32[]{:S(2)}) copy-start(bf16[16,2,16,1536]{3,2,1,0:T(8,128)(2,1)} %down_ref) | copy-start | bytes 4718596
  26.2 1.1 %copy-start.4 = (bf16[2,32,1536]{2,1,0:T(8,128)(2,1)S(1)}, bf16[2,32,1536]{2,1,0:T(8,128)(2,1)}, u32[]{:S(2)}) copy-start(bf16[2,32,1536]{2,1,0:T(8,128)(2,1)} %param.11) | copy-start | bytes 589828
  29.1 9.0 %collective-permute-start.98 = (bf16[32,4096]{1,0:T(8,128)(2,1)S(1)}, bf16[32,4096]{1,0:T(8,128)(2,1)S(1)}, u32[]{:S(2)}, u32[]{:S(2)}) collective-permute-start(bf16[32,4096]{1,0:T(8,128)(2,1)S(1)} %get-tuple-element.490), channel_id=1, source_target_pairs={{4,8},{8,4},{5,9},{9,5},{6,10},{10,6},{7,11},{11,7},{20,24},{24,20... | collective-permute-start | bytes 786440 | tf_op jit(solution)/shard_map/ppermute | solution.py:519
  29.8 3.5 %collective-permute-start.95 = (f32[32,512]{1,0:T(8,128)S(1)}, f32[32,512]{1,0:T(8,128)S(1)}, u32[]{:S(2)}, u32[]{:S(2)}) collective-permute-start(f32[32,512]{1,0:T(8,128)S(1)} %get-tuple-element.488.own_ref), channel_id=1, source_target_pairs={{0,1},{1,0},{2,3},{3,2},{4,5},{5,4},{6,7},{7,6},{8,9},{9,8},{10,11... | collective-permute-start | bytes 196616 | tf_op jit(solution)/shard_map/ppermute | solution.py:518
  29.9 5.3 %collective-permute-start.96 = (f32[32,512]{1,0:T(8,128)S(1)}, f32[32,512]{1,0:T(8,128)S(1)}, u32[]{:S(2)}, u32[]{:S(2)}) collective-permute-start(f32[32,512]{1,0:T(8,128)S(1)} %get-tuple-element.488.own_ref), channel_id=1, source_target_pairs={{0,2},{1,3},{2,0},{3,1},{4,6},{5,7},{6,4},{7,5},{8,10},{9,11},{10,... | collective-permute-start | bytes 196616 | tf_op jit(solution)/shard_map/ppermute | solution.py:518
  32.5 4.0 %collective-permute-start.97 = (f32[32,512]{1,0:T(8,128)S(1)}, f32[32,512]{1,0:T(8,128)S(1)}, u32[]{:S(2)}, u32[]{:S(2)}) collective-permute-start(f32[32,512]{1,0:T(8,128)S(1)} %get-tuple-element.488.own_ref), channel_id=1, source_target_pairs={{0,3},{1,2},{2,1},{3,0},{4,7},{5,6},{6,5},{7,4},{8,11},{9,10},{10,... | collective-permute-start | bytes 196616 | tf_op jit(solution)/shard_map/ppermute | solution.py:518
  36.6 1.6 %copy-start.5 = (bf16[2,32,2,2,4096]{4,3,2,1,0:T(2,128)(2,1)S(1)}, bf16[2,32,2,2,4096]{4,3,2,1,0:T(2,128)(2,1)}, u32[]{:S(2)}) copy-start(bf16[2,32,2,2,4096]{4,3,2,1,0:T(2,128)(2,1)} %param.12) | copy-start | bytes 6291460
  38.2 14.9 %collective-permute-start.15 = (bf16[48,4096]{1,0:T(8,128)(2,1)S(1)}, bf16[48,4096]{1,0:T(8,128)(2,1)S(1)}, u32[]{:S(2)}, u32[]{:S(2)}) collective-permute-start(bf16[48,4096]{1,0:T(8,128)(2,1)S(1)} %get-tuple-element.270), channel_id=1, source_target_pairs={{0,4},{4,0},{8,12},{12,8},{1,5},{5,1},{9,13},{13,9},{2,6},{6,2},{1... | collective-permute-start | bytes 1179656 | tf_op jit(solution)/shard_map/cond/branch_1_fun/ppermute | solution.py:559
  41.5 11.6 %collective-permute-start.16 = (bf16[48,4096]{1,0:T(8,128)(2,1)S(1)}, bf16[48,4096]{1,0:T(8,128)(2,1)S(1)}, u32[]{:S(2)}, u32[]{:S(2)}) collective-permute-start(bf16[48,4096]{1,0:T(8,128)(2,1)S(1)} %get-tuple-element.273), channel_id=1, source_target_pairs={{4,8},{8,4},{5,9},{9,5},{6,10},{10,6},{7,11},{11,7},{20,24},{24,20... | collective-permute-start | bytes 1179656 | tf_op jit(solution)/shard_map/cond/branch_1_fun/ppermute | solution.py:558
  43.8 16.1 %collective-permute-start.13 = (bf16[48,4096]{1,0:T(8,128)(2,1)S(1)}, bf16[48,4096]{1,0:T(8,128)(2,1)S(1)}, u32[]{:S(2)}, u32[]{:S(2)}) collective-permute-start(bf16[48,4096]{1,0:T(8,128)(2,1)S(1)} %get-tuple-element.258), channel_id=1, source_target_pairs={{0,4},{4,0},{8,12},{12,8},{1,5},{5,1},{9,13},{13,9},{2,6},{6,2},{1... | collective-permute-start | bytes 1179656 | tf_op jit(solution)/shard_map/cond/branch_1_fun/ppermute | solution.py:559
  47.1 12.7 %collective-permute-start.18 = (bf16[48,4096]{1,0:T(8,128)(2,1)S(1)}, bf16[48,4096]{1,0:T(8,128)(2,1)S(1)}, u32[]{:S(2)}, u32[]{:S(2)}) collective-permute-start(bf16[48,4096]{1,0:T(8,128)(2,1)S(1)} %get-tuple-element.275), channel_id=1, source_target_pairs={{4,8},{8,4},{5,9},{9,5},{6,10},{10,6},{7,11},{11,7},{20,24},{24,20... | collective-permute-start | bytes 1179656 | tf_op jit(solution)/shard_map/cond/branch_1_fun/ppermute | solution.py:558
  55.1 13.1 %collective-permute-start.17 = (bf16[48,4096]{1,0:T(8,128)(2,1)S(1)}, bf16[48,4096]{1,0:T(8,128)(2,1)S(1)}, u32[]{:S(2)}, u32[]{:S(2)}) collective-permute-start(bf16[48,4096]{1,0:T(8,128)(2,1)S(1)} %get-tuple-element.274), channel_id=1, source_target_pairs={{0,4},{4,0},{8,12},{12,8},{1,5},{5,1},{9,13},{13,9},{2,6},{6,2},{1... | collective-permute-start | bytes 1179656 | tf_op jit(solution)/shard_map/cond/branch_1_fun/ppermute | solution.py:559
  57.4 10.8 %collective-permute-start.20 = (bf16[48,4096]{1,0:T(8,128)(2,1)S(1)}, bf16[48,4096]{1,0:T(8,128)(2,1)S(1)}, u32[]{:S(2)}, u32[]{:S(2)}) collective-permute-start(bf16[48,4096]{1,0:T(8,128)(2,1)S(1)} %get-tuple-element.277), channel_id=1, source_target_pairs={{4,8},{8,4},{5,9},{9,5},{6,10},{10,6},{7,11},{11,7},{20,24},{24,20... | collective-permute-start | bytes 1179656 | tf_op jit(solution)/shard_map/cond/branch_1_fun/ppermute | solution.py:558
  61.9 14.8 %collective-permute-start.19 = (bf16[48,4096]{1,0:T(8,128)(2,1)S(1)}, bf16[48,4096]{1,0:T(8,128)(2,1)S(1)}, u32[]{:S(2)}, u32[]{:S(2)}) collective-permute-start(bf16[48,4096]{1,0:T(8,128)(2,1)S(1)} %get-tuple-element.276), channel_id=1, source_target_pairs={{0,4},{4,0},{8,12},{12,8},{1,5},{5,1},{9,13},{13,9},{2,6},{6,2},{1... | collective-permute-start | bytes 1179656 | tf_op jit(solution)/shard_map/cond/branch_1_fun/ppermute | solution.py:559
  65.8 10.8 %collective-permute-start.22 = (bf16[48,4096]{1,0:T(8,128)(2,1)S(1)}, bf16[48,4096]{1,0:T(8,128)(2,1)S(1)}, u32[]{:S(2)}, u32[]{:S(2)}) collective-permute-start(bf16[48,4096]{1,0:T(8,128)(2,1)S(1)} %get-tuple-element.279), channel_id=1, source_target_pairs={{4,8},{8,4},{5,9},{9,5},{6,10},{10,6},{7,11},{11,7},{20,24},{24,20... | collective-permute-start | bytes 1179656 | tf_op jit(solution)/shard_map/cond/branch_1_fun/ppermute | solution.py:558
  70.3 14.8 %collective-permute-start.21 = (bf16[48,4096]{1,0:T(8,128)(2,1)S(1)}, bf16[48,4096]{1,0:T(8,128)(2,1)S(1)}, u32[]{:S(2)}, u32[]{:S(2)}) collective-permute-start(bf16[48,4096]{1,0:T(8,128)(2,1)S(1)} %get-tuple-element.278), channel_id=1, source_target_pairs={{0,4},{4,0},{8,12},{12,8},{1,5},{5,1},{9,13},{13,9},{2,6},{6,2},{1... | collective-permute-start | bytes 1179656 | tf_op jit(solution)/shard_map/cond/branch_1_fun/ppermute | solution.py:559
  74.3 10.8 %collective-permute-start.24 = (bf16[48,4096]{1,0:T(8,128)(2,1)S(1)}, bf16[48,4096]{1,0:T(8,128)(2,1)S(1)}, u32[]{:S(2)}, u32[]{:S(2)}) collective-permute-start(bf16[48,4096]{1,0:T(8,128)(2,1)S(1)} %get-tuple-element.281), channel_id=1, source_target_pairs={{4,8},{8,4},{5,9},{9,5},{6,10},{10,6},{7,11},{11,7},{20,24},{24,20... | collective-permute-start | bytes 1179656 | tf_op jit(solution)/shard_map/cond/branch_1_fun/ppermute | solution.py:558
  75.1 26.5 %collective-permute-start.14 = (bf16[64,4096]{1,0:T(8,128)(2,1)S(1)}, bf16[64,4096]{1,0:T(8,128)(2,1)S(1)}, u32[]{:S(2)}, u32[]{:S(2)}) collective-permute-start(bf16[64,4096]{1,0:T(8,128)(2,1)S(1)} %branch_1_fun.12.mine_ref), channel_id=1, source_target_pairs={{0,16},{16,0},{1,17},{17,1},{2,18},{18,2},{3,19},{19,3},{4,20},{20... | collective-permute-start | bytes 1572872 | tf_op jit(solution)/shard_map/cond/branch_1_fun/ppermute | solution.py:566
  78.9 14.7 %collective-permute-start.23 = (bf16[48,4096]{1,0:T(8,128)(2,1)S(1)}, bf16[48,4096]{1,0:T(8,128)(2,1)S(1)}, u32[]{:S(2)}, u32[]{:S(2)}) collective-permute-start(bf16[48,4096]{1,0:T(8,128)(2,1)S(1)} %get-tuple-element.280), channel_id=1, source_target_pairs={{0,4},{4,0},{8,12},{12,8},{1,5},{5,1},{9,13},{13,9},{2,6},{6,2},{1... | collective-permute-start | bytes 1179656 | tf_op jit(solution)/shard_map/cond/branch_1_fun/ppermute | solution.py:559
  82.8 10.7 %collective-permute-start.25 = (bf16[48,4096]{1,0:T(8,128)(2,1)S(1)}, bf16[48,4096]{1,0:T(8,128)(2,1)S(1)}, u32[]{:S(2)}, u32[]{:S(2)}) collective-permute-start(bf16[48,4096]{1,0:T(8,128)(2,1)S(1)} %get-tuple-element.282), channel_id=1, source_target_pairs={{4,8},{8,4},{5,9},{9,5},{6,10},{10,6},{7,11},{11,7},{20,24},{24,20... | collective-permute-start | bytes 1179656 | tf_op jit(solution)/shard_map/cond/branch_1_fun/ppermute | solution.py:558
  87.4 14.1 %collective-permute-start.26 = (bf16[48,4096]{1,0:T(8,128)(2,1)S(1)}, bf16[48,4096]{1,0:T(8,128)(2,1)S(1)}, u32[]{:S(2)}, u32[]{:S(2)}) collective-permute-start(bf16[48,4096]{1,0:T(8,128)(2,1)S(1)} %get-tuple-element.283), channel_id=1, source_target_pairs={{0,4},{4,0},{8,12},{12,8},{1,5},{5,1},{9,13},{13,9},{2,6},{6,2},{1... | collective-permute-start | bytes 1179656 | tf_op jit(solution)/shard_map/cond/branch_1_fun/ppermute | solution.py:559
  91.4 10.1 %collective-permute-start.27 = (bf16[48,4096]{1,0:T(8,128)(2,1)S(1)}, bf16[48,4096]{1,0:T(8,128)(2,1)S(1)}, u32[]{:S(2)}, u32[]{:S(2)}) collective-permute-start(bf16[48,4096]{1,0:T(8,128)(2,1)S(1)} %get-tuple-element.284), channel_id=1, source_target_pairs={{4,8},{8,4},{5,9},{9,5},{6,10},{10,6},{7,11},{11,7},{20,24},{24,20... | collective-permute-start | bytes 1179656 | tf_op jit(solution)/shard_map/cond/branch_1_fun/ppermute | solution.py:558
  106.1 1.0 copy-start.6
  107.0 0.9 copy-start.1
where the time goes:
time: 110 us; the launch traced here: 108 us
  starting transfers between devices  52.1 us (47%)
  Pallas kernels  31.9 us (29%)
  waiting for transfers between devices  15.6 us (14%)
  local copies, waits for them, and re-layouts  6.79 us (6%)
    pallas_call x16, Pallas kernels, kernel(): pl.pallas_call(body, out_shape=[jax.ShapeDtypeStruct(shape, dtype) for sh...  31.9 us
    ppermute x7, starting transfers between devices, flow(): got_outer.append(lax.ppermute(outer, 'dp', outer_pairs))  24.9 us
    ppermute x7, waiting for transfers between devices, flow(): got_outer.append(lax.ppermute(outer, 'dp', outer_pairs))  9.87 us
    ppermute x3, starting transfers between devices, turn(): lax.ppermute(x, 'dp', [(i, (i + shift) % count) for i in range(count)])  7.03 us
    unnamed x15, local copies, waits for them, and re-layouts  5.68 us
    ppermute x7, starting transfers between devices, flow(): got_middle.append(lax.ppermute(middle, 'dp', middle_pair))  4.72 us
    ppermute x1, starting transfers between devices, on_device(): lax.ppermute(jnp.concatenate([near, beside], axis=0), 'expert', [(0, 1),...  4.48 us
    ppermute x3, waiting for transfers between devices, relayed(): lax.ppermute(part, ('expert', 'pair'), [(i, i ^ mask) for i in range(4)])  3.27 us
  transfers between devices with their start and end apart: 27, of which 9 were waited for; matrix products, arithmetic and copies ran while one was open for 0% of the time, Pallas kernels for 24%

commit v1 on v0

--- a/solution.py
+++ b/solution.py
@@ -111,7 +111,8 @@
 GAP = LAG * CHUNK
 ROW_STEP = 8
 MAGNITUDE_ROWS = 16
-QUEUE_ROWS = (144, 168, 192, 216)
+QUEUE_ROWS = (160, 168, 184, 208)
+LONG_ROWS = 208
 
 
 def chunk_rows(total):
@@ -273,11 +274,12 @@
     panel_of = (lax.broadcasted_iota(jnp.int32, (panels * 2 * rank, routes), 0) // (2 * rank)).astype(jnp.float32)
     join_ref[:panels, :] = beside_ref[...]
     join_ref[panels:, :] = half_ref[...]
-    for s, state_ref in enumerate(state_refs):
-        one = state_ref[...]
+    lows = nt_dot(down, jnp.concatenate([state_ref[...] for state_ref in state_refs], axis=0))
+    rows = routes // 2
+    for s in range(len(state_refs)):
         cols = slice(s * routes, (s + 1) * routes)
-        low = nt_dot(down, jnp.concatenate([one, one], axis=0))
-        low = jnp.where(panel_of == info_ref[0:1, cols], low, 0.0)
+        low = lows[:, s * rows : (s + 1) * rows]
+        low = jnp.where(panel_of == info_ref[0:1, cols], jnp.concatenate([low, low], axis=1), 0.0)
         part_ref[:, cols] = jnp.sum(low.reshape(panels, 2 * rank, routes), axis=0)
 
 
@@ -365,7 +367,7 @@
         out_ref[2 * depth :] = across_ref[...]
 
 
-def relay_chunk_kernel(first, count, known, lhs_ref, forward_ref, up_ref, *refs):
+def relay_chunk_kernel(first, count, known, tile, lhs_ref, forward_ref, up_ref, *refs):
     came, out_refs = refs[:-2], refs[-2:]
     here = slice(2 * first, 2 * (first + count))
 
@@ -378,10 +380,10 @@
             passed = jnp.dot(forward_ref[way, here, : 2 * known], rows, preferred_element_type=jnp.float32)
             out_refs[way][:, cols] = (delta[2 * way * count : 2 * (way + 1) * count] + passed).astype(jnp.bfloat16)
 
-    column_tiles(up_ref.shape[1], body)
-
-
-def relay_pick_kernel(known, arrive_ref, local_ref, up_ref, *refs):
+    column_tiles(up_ref.shape[1], body, tile)
+
+
+def relay_pick_kernel(known, tile, arrive_ref, local_ref, up_ref, *refs):
     came, out_ref = refs[:-1], refs[-1]
     routes = out_ref.shape[1]
 
@@ -395,7 +397,7 @@
         for p in range(2):
             out_ref[p, :, cols] = delta[p * routes : (p + 1) * routes].astype(out_ref.dtype)
 
-    column_tiles(up_ref.shape[1], body)
+    column_tiles(up_ref.shape[1], body, tile)
 
 
 def relay_gate_kernel(
@@ -427,7 +429,7 @@
         for k in range(2):
             out_ref[:, k, cols] = hidden[k * rows : (k + 1) * rows]
 
-    column_tiles(out_ref.shape[2], body)
+    column_tiles(out_ref.shape[2], body, 1024)
 
 
 def relay_base_kernel(base_ref, out_ref):
@@ -532,6 +534,7 @@
         (outer_first, middle_first, first, held, info, lows, forward, up_rows) = operands[:8]
         arrive, panel, base, half, beside, across = operands[8:]
         chunks = chunk_rows(total)
+        tile = 512 if total < LONG_ROWS else 256
         got_outer, got_middle = [], []
         for k, (start, size) in enumerate(chunks):
             if k == 0:
@@ -550,7 +553,7 @@
                     )
                 known = k + 1 - LAG
                 outer, middle = kernel(
-                    functools.partial(relay_chunk_kernel, start, size, chunks[known][0]),
+                    functools.partial(relay_chunk_kernel, start, size, chunks[known][0], tile),
                     [lhs, forward, up_rows, *got_outer[:known], *got_middle[:known]],
                     [((2 * size, hidden), bf16)] * 2,
                     cost=4 + k,
@@ -566,7 +569,7 @@
         other = lax.ppermute(mine, "groups", [(0, 1), (1, 0)])
         last, size = chunks[-1]
         [picked] = kernel(
-            functools.partial(relay_pick_kernel, last),
+            functools.partial(relay_pick_kernel, last, tile),
             [arrive, local, up_rows, *got_outer[:-1], *got_middle[:-1]],
             [((2, routes, hidden), bf16)],
         )
@@ -605,16 +608,15 @@
 
     if (count, lax.axis_size("expert"), lax.axis_size("pair")) == (4, 2, 2):
         one = states.reshape(steps * rows, width)
-        flat = route_panels.transpose(2, 0, 1).reshape(1, routes)
-        number = jnp.concatenate([flat // panels, flat % panels], axis=0).astype(bf16)
-        number = jnp.pad(number, ((0, ROW_TILE - 2), (0, 0)))
         which = 2 * lax.axis_index("expert") + lax.axis_index("pair")
-        one, number = lax.optimization_barrier((one, number))
         far = [(4 * d + e, 4 * ((d + e) % count) + e) for d in range(count) for e in range(4)]
-        near = lax.ppermute(number, ("dp", "expert", "pair"), far)
+        near = lax.ppermute(route_panels, ("dp", "expert", "pair"), far)
+        one, near = lax.optimization_barrier((one, near))
+        flat = near.transpose(2, 0, 1).reshape(1, routes)
+        near = jnp.concatenate([flat // panels, flat % panels], axis=0).astype(bf16)
+        near = jnp.pad(near, ((0, ROW_TILE - 2), (0, 0)))
         beside = lax.ppermute(near, "pair", [(0, 1), (1, 0)])
         both = lax.ppermute(jnp.concatenate([near, beside], axis=0), "expert", [(0, 1), (1, 0)])
-        one, near = lax.optimization_barrier((one, near))
         seen = [one] + [turn(one, s) for s in range(1, count)]
         return relayed(seen, [near, beside, both], which, magnitude, base, down, up)
 

time: 110 us -> 107 us (0.973)
  Pallas kernels: 31.9 us -> 29.9 us
    ppermute x1, starting transfers between devices: 0.74 us -> 3.09 us  [relayed(): beside = lax.ppermute(half, 'dp', outer_pairs)]
    ppermute x1, starting transfers between devices: 3 us -> 0.7 us  [on_device(): beside = lax.ppermute(near, 'pair', [(0, 1), (1, 0)])]
    pallas_call x16, Pallas kernels: 31.9 us -> 29.9 us  [kernel(): pl.pallas_call(body, out_shape=[jax.ShapeDtypeStruct(shape, dtype) for sh...]
    ppermute x7, starting transfers between devices: 24.9 us -> 26.6 us  [flow(): got_outer.append(lax.ppermute(outer, 'dp', outer_pairs))]
    ppermute x3, starting transfers between devices: 7.03 us -> 5.51 us  [turn(): lax.ppermute(x, 'dp', [(i, (i + shift) % count) for i in range(count)])]
  transfers between devices with their start and end apart: 27 -> 27, of which waited for: 9 -> 9; matrix products, arithmetic and copies ran while one was open for 0% -> 1% of each run, Pallas kernels for 24% -> 25%
where the time goes in v1:
time: 107 us; the launch traced here: 106 us
  starting transfers between devices  52.4 us (49%)
  Pallas kernels  29.9 us (28%)
  waiting for transfers between devices  15.8 us (15%)
  local copies, waits for them, and re-layouts  6.07 us (6%)
    pallas_call x16, Pallas kernels, kernel(): pl.pallas_call(body, out_shape=[jax.ShapeDtypeStruct(shape, dtype) for sh...  29.9 us
    ppermute x7, starting transfers between devices, flow(): got_outer.append(lax.ppermute(outer, 'dp', outer_pairs))  26.6 us
    ppermute x7, waiting for transfers between devices, flow(): got_outer.append(lax.ppermute(outer, 'dp', outer_pairs))  9.89 us
    unnamed x15, local copies, waits for them, and re-layouts  5.68 us
    ppermute x3, starting transfers between devices, turn(): lax.ppermute(x, 'dp', [(i, (i + shift) % count) for i in range(count)])  5.51 us
    ppermute x7, starting transfers between devices, flow(): got_middle.append(lax.ppermute(middle, 'dp', middle_pair))  4.72 us
    ppermute x1, starting transfers between devices, on_device(): lax.ppermute(jnp.concatenate([near, beside], axis=0), 'expert', [(0, 1),...  4.33 us
    ppermute x3, waiting for transfers between devices, relayed(): lax.ppermute(part, ('expert', 'pair'), [(i, i ^ mask) for i in range(4)])  3.4 us
  transfers between devices with their start and end apart: 27, of which 9 were waited for; matrix products, arithmetic and copies ran while one was open for 1% of the time, Pallas kernels for 25%

profile of v1, /device:TPU:0, one launch (start us, length us, event | category | flops | bytes accessed | tf_op | source)
XLA Modules:
  0.0 105.6 jit_solution(1767154954339922025)
XLA Ops:
  0.0 1.5 %collective-permute-start.89 = (s32[2,32,2]{1,2,0:T(2,128)}, s32[2,32,2]{1,2,0:T(2,128)S(1)}, u32[]{:S(2)}, u32[]{:S(2)}) collective-permute-start(s32[2,32,2]{1,2,0:T(2,128)} %param.13), channel_id=1, source_target_pairs={{0,0},{1,5},{2,10},{3,15},{4,4},{5,9},{6,14},{7,3},{8,8},{9,13},{1... | collective-permute-start | bytes 1544 | tf_op jit(solution)/shard_map/ppermute | solution.py:613
  1.9 3.1 %collective-permute-start.96 = (bf16[16,4096]{1,0:T(8,128)(2,1)S(1)}, bf16[16,4096]{1,0:T(8,128)(2,1)S(1)}, u32[]{:S(2)}, u32[]{:S(2)}) collective-permute-start(bf16[16,4096]{1,0:T(8,128)(2,1)S(1)} %bitcast.35), channel_id=1, source_target_pairs={{0,4},{4,0},{8,12},{12,8},{1,5},{5,1},{9,13},{13,9},{2,6},{6,2},{1... | collective-permute-start | bytes 393224 | tf_op jit(solution)/shard_map/ppermute | solution.py:479
  5.1 3.0 %collective-permute-start.94 = (bf16[64,1536]{1,0:T(8,128)(2,1)}, bf16[64,1536]{1,0:T(8,128)(2,1)S(1)}, u32[]{:S(2)}, u32[]{:S(2)}) collective-permute-start(bf16[64,1536]{1,0:T(8,128)(2,1)} %bitcast.27), channel_id=1, source_target_pairs={{0,8},{4,12},{8,0},{12,4},{1,9},{5,13},{9,1},{13,5},{2,10},{6,14},... | collective-permute-start | bytes 589832 | tf_op jit(solution)/shard_map/ppermute | solution.py:607
  8.1 2.5 %collective-permute-start.95 = (bf16[64,1536]{1,0:T(8,128)(2,1)}, bf16[64,1536]{1,0:T(8,128)(2,1)S(1)}, u32[]{:S(2)}, u32[]{:S(2)}) collective-permute-start(bf16[64,1536]{1,0:T(8,128)(2,1)} %bitcast.28), channel_id=1, source_target_pairs={{0,12},{4,0},{8,4},{12,8},{1,13},{5,1},{9,5},{13,9},{2,14},{6,2},{... | collective-permute-start | bytes 589832 | tf_op jit(solution)/shard_map/ppermute | solution.py:607
  10.7 0.7 collective-permute-start.90
  11.4 0.8 collective-permute-done.90.refs_1_
  12.2 4.3 %collective-permute-start.91 = (bf16[32,128]{1,0:T(8,128)(2,1)S(1)}, bf16[32,128]{1,0:T(8,128)(2,1)S(1)}, u32[]{:S(2)}, u32[]{:S(2)}) collective-permute-start(bf16[32,128]{1,0:T(8,128)(2,1)S(1)} %pad_maximum_fusion), channel_id=1, source_target_pairs={{0,2},{2,0},{1,3},{3,1},{4,6},{6,4},{5,7},{7,5},{8,10},{10,8},{9,1... | collective-permute-start | bytes 24584 | tf_op jit(solution)/shard_map/ppermute | solution.py:619
  16.5 1.6 %collective-permute-done.91.refs_2_ = bf16[32,128]{1,0:T(8,128)(2,1)S(1)} collective-permute-done((bf16[32,128]{1,0:T(8,128)(2,1)S(1)}, bf16[32,128]{1,0:T(8,128)(2,1)S(1)}, u32[]{:S(2)}, u32[]{:S(2)}) %collective-permute-start.91) | collective-permute-done | bytes 8224 | tf_op jit(solution)/shard_map/ppermute | solution.py:619
  18.1 1.3 %shard_map.69 = (f32[16,512]{1,0:T(8,128)S(1)}, f32[8,128]{1,0:T(8,128)S(1)}, bf16[2,512,512]{2,1,0:T(8,128)(2,1)S(1)}, bf16[192,512]{1,0:T(8,128)(2,1)S(1)}, bf...) custom-call(s32[1]{0:T(128)} %bitcast.15.me_ref, s32[1]{0:T(128)} %bitcast.16.part_ref, ...), custom_call_target="tpu_custom_call" | custom-call | bytes 134217728 | tf_op jit(solution)/shard_map/pallas_call | solution.py:466
  19.4 1.6 %collective-permute-start.92 = (f32[8,128]{1,0:T(8,128)S(1)}, f32[8,128]{1,0:T(8,128)S(1)}, u32[]{:S(2)}, u32[]{:S(2)}) collective-permute-start(f32[8,128]{1,0:T(8,128)S(1)} %get-tuple-element.474.own_ref), channel_id=1, source_target_pairs={{0,16},{16,0},{1,17},{17,1},{2,18},{18,2},{3,19},{19,3},{4,20},{20... | collective-permute-start | bytes 12296 | tf_op jit(solution)/shard_map/ppermute | solution.py:507
  21.0 2.2 %copy-done.2 = bf16[16,2,16,4096]{3,2,1,0:T(8,128)(2,1)S(1)} copy-done((bf16[16,2,16,4096]{3,2,1,0:T(8,128)(2,1)S(1)}, bf16[16,2,16,4096]{3,2,1,0:T(8,128)(2,1)}, u32[]{:S(2)}) %copy-start.2) | copy-done | bytes 4194328
  23.2 1.4 %copy-done.3 = bf16[16,2,16,1536]{3,2,1,0:T(8,128)(2,1)S(1)} copy-done((bf16[16,2,16,1536]{3,2,1,0:T(8,128)(2,1)S(1)}, bf16[16,2,16,1536]{3,2,1,0:T(8,128)(2,1)}, u32[]{:S(2)}) %copy-start.3) | copy-done | bytes 1572888
  25.8 0.7 shard_map.72
  26.5 0.7 collective-permute-start.100
  27.2 2.1 %collective-permute-start.98 = (f32[32,512]{1,0:T(8,128)S(1)}, f32[32,512]{1,0:T(8,128)S(1)}, u32[]{:S(2)}, u32[]{:S(2)}) collective-permute-start(f32[32,512]{1,0:T(8,128)S(1)} %get-tuple-element.486.own_ref), channel_id=1, source_target_pairs={{0,2},{1,3},{2,0},{3,1},{4,6},{5,7},{6,4},{7,5},{8,10},{9,11},{10,... | collective-permute-start | bytes 196616 | tf_op jit(solution)/shard_map/ppermute | solution.py:520
  30.0 2.0 %collective-permute-done.98.far_ref = f32[32,512]{1,0:T(8,128)S(1)} collective-permute-done((f32[32,512]{1,0:T(8,128)S(1)}, f32[32,512]{1,0:T(8,128)S(1)}, u32[]{:S(2)}, u32[]{:S(2)}) %collective-permute-start.98) | collective-permute-done | bytes 65568 | tf_op jit(solution)/shard_map/ppermute | solution.py:520
  32.0 1.4 %collective-permute-done.99.diag_ref = f32[32,512]{1,0:T(8,128)S(1)} collective-permute-done((f32[32,512]{1,0:T(8,128)S(1)}, f32[32,512]{1,0:T(8,128)S(1)}, u32[]{:S(2)}, u32[]{:S(2)}) %collective-permute-start.99) | collective-permute-done | bytes 65568 | tf_op jit(solution)/shard_map/ppermute | solution.py:520
  33.4 1.6 %shard_map.73 = (bf16[48,4096]{1,0:T(8,128)(2,1)S(1)}, bf16[48,4096]{1,0:T(8,128)(2,1)S(1)}) custom-call(bf16[192,512]{1,0:T(8,128)(2,1)S(1)} %get-tuple-element.477.first_ref, bf16[192,512]{1,0:T(8,128)(2,1)S(1)} %get-tuple-element.478.held_ref, f32[32,512]{1,0:T(8,128)S(1)} %get-tuple-element.486.own_ref, f32[32,512]{1,0:T(8,128)S(1)} %collective-permute-done.97.core_ref, ...), custom_call_target="tpu_custom_call" | custom-call | bytes 1048576 | tf_op jit(solution)/shard_map/pallas_call | solution.py:466
  35.0 68.7 %conditional.1 = (bf16[2,32,2,4096]{3,2,1,0:T(2,128)(2,1)S(1)}) conditional(s32[]{:T(128)} %bitcast.21, (s32[]{:T(128)}, s32[]{:T(128)}, bf16[192,512]{1,0:T(8,128)(2,1)S(1)}, bf16[192,512]{1,0:T(8,128)(2,1)S(1)}, f32[32,512]{1,0:T(8,128)S(1)}, /*index=5*/f32[32,512]{1,0:T(8,128)S(1)}, f32[32,512]{1,0:T(8,128)S(1)}, ...), branch_computations={%region_0.1_spmd, %region_1.2_spmd, %region_2.3_spmd, %region_3.4_... | conditional | bytes 136315808 | solution.py:590
  35.0 5.0 %collective-permute-start.17 = (bf16[48,4096]{1,0:T(8,128)(2,1)S(1)}, bf16[48,4096]{1,0:T(8,128)(2,1)S(1)}, u32[]{:S(2)}, u32[]{:S(2)}) collective-permute-start(bf16[48,4096]{1,0:T(8,128)(2,1)S(1)} %get-tuple-element.272), channel_id=1, source_target_pairs={{0,4},{4,0},{8,12},{12,8},{1,5},{5,1},{9,13},{13,9},{2,6},{6,2},{1... | collective-permute-start | bytes 1179656 | tf_op jit(solution)/shard_map/cond/branch_1_fun/ppermute | solution.py:562
  40.0 0.7 collective-permute-start.18
  40.7 1.6 %branch_1_fun.11 = (bf16[48,4096]{1,0:T(8,128)(2,1)S(1)}, bf16[48,4096]{1,0:T(8,128)(2,1)S(1)}) custom-call(bf16[192,512]{1,0:T(8,128)(2,1)S(1)} %get-tuple-element.253.first_ref, bf16[192,512]{1,0:T(8,128)(2,1)S(1)} %get-tuple-element.254.held_ref, f32[32,512]{1,0:T(8,128)S(1)} %get-tuple-element.267.own_ref, f32[32,512]{1,0:T(8,128)S(1)} %get-tuple-element.268.core_ref, ...), custom_call_target="tpu_custom_call" | custom-call | bytes 1048576 | tf_op jit(solution)/shard_map/cond/branch_1_fun/pallas_call | solution.py:466
  42.2 3.3 %collective-permute-start.15 = (bf16[48,4096]{1,0:T(8,128)(2,1)S(1)}, bf16[48,4096]{1,0:T(8,128)(2,1)S(1)}, u32[]{:S(2)}, u32[]{:S(2)}) collective-permute-start(bf16[48,4096]{1,0:T(8,128)(2,1)S(1)} %get-tuple-element.260), channel_id=1, source_target_pairs={{0,4},{4,0},{8,12},{12,8},{1,5},{5,1},{9,13},{13,9},{2,6},{6,2},{1... | collective-permute-start | bytes 1179656 | tf_op jit(solution)/shard_map/cond/branch_1_fun/ppermute | solution.py:562
  45.6 0.7 collective-permute-start.20
  46.3 4.5 %branch_1_fun.13.base_ref = bf16[2,128,4096]{2,1,0:T(8,128)(2,1)S(1)} custom-call(bf16[64,2,2,4096]{3,2,1,0:T(2,128)(2,1)S(1)} %get-tuple-element.263.base_ref), custom_call_target="tpu_custom_call" | custom-call | bytes 1048576 | tf_op jit(solution)/shard_map/cond/branch_1_fun/pallas_call | solution.py:466
  50.7 0.8 branch_1_fun.14
  51.6 2.0 %branch_1_fun.15 = (bf16[48,4096]{1,0:T(8,128)(2,1)S(1)}, bf16[48,4096]{1,0:T(8,128)(2,1)S(1)}) custom-call(bf16[2,512,512]{2,1,0:T(8,128)(2,1)S(1)} %get-tuple-element.273.lhs_ref, bf16[2,512,512]{2,1,0:T(8,128)(2,1)S(1)} %get-tuple-element.274.forward_ref, bf16[512,4096]{1,0:T(8,128)(2,1)S(1)} %get-tuple-element.259.up_ref, ...), custom_call_target="tpu_custom_call" | custom-call | bytes 6291456 | tf_op jit(solution)/shard_map/cond/branch_1_fun/pallas_call | solution.py:466
  53.6 2.3 %collective-permute-start.19 = (bf16[48,4096]{1,0:T(8,128)(2,1)S(1)}, bf16[48,4096]{1,0:T(8,128)(2,1)S(1)}, u32[]{:S(2)}, u32[]{:S(2)}) collective-permute-start(bf16[48,4096]{1,0:T(8,128)(2,1)S(1)} %get-tuple-element.276), channel_id=1, source_target_pairs={{0,4},{4,0},{8,12},{12,8},{1,5},{5,1},{9,13},{13,9},{2,6},{6,2},{1... | collective-permute-start | bytes 1179656 | tf_op jit(solution)/shard_map/cond/branch_1_fun/ppermute | solution.py:562
  56.6 1.7 %collective-permute-done.15.second_ref.refs_1_ = bf16[48,4096]{1,0:T(8,128)(2,1)S(1)} collective-permute-done((bf16[48,4096]{1,0:T(8,128)(2,1)S(1)}, bf16[48,4096]{1,0:T(8,128)(2,1)S(1)}, u32[]{:S(2)}, u32[]{:S(2)}) %collective-permute-start.15) | collective-permute-done | bytes 393248 | tf_op jit(solution)/shard_map/cond/branch_1_fun/ppermute | solution.py:562
  58.3 2.0 %branch_1_fun.16 = (bf16[48,4096]{1,0:T(8,128)(2,1)S(1)}, bf16[48,4096]{1,0:T(8,128)(2,1)S(1)}) custom-call(bf16[2,512,512]{2,1,0:T(8,128)(2,1)S(1)} %get-tuple-element.273.lhs_ref, bf16[2,512,512]{2,1,0:T(8,128)(2,1)S(1)} %get-tuple-element.274.forward_ref, bf16[512,4096]{1,0:T(8,128)(2,1)S(1)} %get-tuple-element.259.up_ref, ...), custom_call_target="tpu_custom_call" | custom-call | bytes 7340032 | tf_op jit(solution)/shard_map/cond/branch_1_fun/pallas_call | solution.py:466
  60.3 4.0 %collective-permute-start.21 = (bf16[48,4096]{1,0:T(8,128)(2,1)S(1)}, bf16[48,4096]{1,0:T(8,128)(2,1)S(1)}, u32[]{:S(2)}, u32[]{:S(2)}) collective-permute-start(bf16[48,4096]{1,0:T(8,128)(2,1)S(1)} %get-tuple-element.278), channel_id=1, source_target_pairs={{0,4},{4,0},{8,12},{12,8},{1,5},{5,1},{9,13},{13,9},{2,6},{6,2},{1... | collective-permute-start | bytes 1179656 | tf_op jit(solution)/shard_map/cond/branch_1_fun/ppermute | solution.py:562
  64.3 0.7 collective-permute-start.24
  65.0 1.7 %collective-permute-done.19.refs_2_ = bf16[48,4096]{1,0:T(8,128)(2,1)S(1)} collective-permute-done((bf16[48,4096]{1,0:T(8,128)(2,1)S(1)}, bf16[48,4096]{1,0:T(8,128)(2,1)S(1)}, u32[]{:S(2)}, u32[]{:S(2)}) %collective-permute-start.19) | collective-permute-done | bytes 393248 | tf_op jit(solution)/shard_map/cond/branch_1_fun/ppermute | solution.py:562
  66.7 2.1 %branch_1_fun.17 = (bf16[48,4096]{1,0:T(8,128)(2,1)S(1)}, bf16[48,4096]{1,0:T(8,128)(2,1)S(1)}) custom-call(bf16[2,512,512]{2,1,0:T(8,128)(2,1)S(1)} %get-tuple-element.273.lhs_ref, bf16[2,512,512]{2,1,0:T(8,128)(2,1)S(1)} %get-tuple-element.274.forward_ref, bf16[512,4096]{1,0:T(8,128)(2,1)S(1)} %get-tuple-element.259.up_ref, ...), custom_call_target="tpu_custom_call" | custom-call | bytes 8388608 | tf_op jit(solution)/shard_map/cond/branch_1_fun/pallas_call | solution.py:466
  68.8 4.0 %collective-permute-start.23 = (bf16[48,4096]{1,0:T(8,128)(2,1)S(1)}, bf16[48,4096]{1,0:T(8,128)(2,1)S(1)}, u32[]{:S(2)}, u32[]{:S(2)}) collective-permute-start(bf16[48,4096]{1,0:T(8,128)(2,1)S(1)} %get-tuple-element.280), channel_id=1, source_target_pairs={{0,4},{4,0},{8,12},{12,8},{1,5},{5,1},{9,13},{13,9},{2,6},{6,2},{1... | collective-permute-start | bytes 1179656 | tf_op jit(solution)/shard_map/cond/branch_1_fun/ppermute | solution.py:562
  73.5 1.6 %collective-permute-start.16 = (bf16[64,4096]{1,0:T(8,128)(2,1)S(1)}, bf16[64,4096]{1,0:T(8,128)(2,1)S(1)}, u32[]{:S(2)}, u32[]{:S(2)}) collective-permute-start(bf16[64,4096]{1,0:T(8,128)(2,1)S(1)} %branch_1_fun.12.mine_ref), channel_id=1, source_target_pairs={{0,16},{16,0},{1,17},{17,1},{2,18},{18,2},{3,19},{19,3},{4,20},{20... | collective-permute-start | bytes 1572872 | tf_op jit(solution)/shard_map/cond/branch_1_fun/ppermute | solution.py:569
  75.2 2.1 %branch_1_fun.18 = (bf16[48,4096]{1,0:T(8,128)(2,1)S(1)}, bf16[48,4096]{1,0:T(8,128)(2,1)S(1)}) custom-call(bf16[2,512,512]{2,1,0:T(8,128)(2,1)S(1)} %get-tuple-element.273.lhs_ref, bf16[2,512,512]{2,1,0:T(8,128)(2,1)S(1)} %get-tuple-element.274.forward_ref, bf16[512,4096]{1,0:T(8,128)(2,1)S(1)} %get-tuple-element.259.up_ref, ...), custom_call_target="tpu_custom_call" | custom-call | bytes 9437184 | tf_op jit(solution)/shard_map/cond/branch_1_fun/pallas_call | solution.py:466
  77.3 4.0 %collective-permute-start.25 = (bf16[48,4096]{1,0:T(8,128)(2,1)S(1)}, bf16[48,4096]{1,0:T(8,128)(2,1)S(1)}, u32[]{:S(2)}, u32[]{:S(2)}) collective-permute-start(bf16[48,4096]{1,0:T(8,128)(2,1)S(1)} %get-tuple-element.282), channel_id=1, source_target_pairs={{0,4},{4,0},{8,12},{12,8},{1,5},{5,1},{9,13},{13,9},{2,6},{6,2},{1... | collective-permute-start | bytes 1179656 | tf_op jit(solution)/shard_map/cond/branch_1_fun/ppermute | solution.py:562
  82.0 1.6 %collective-permute-done.23.refs_4_ = bf16[48,4096]{1,0:T(8,128)(2,1)S(1)} collective-permute-done((bf16[48,4096]{1,0:T(8,128)(2,1)S(1)}, bf16[48,4096]{1,0:T(8,128)(2,1)S(1)}, u32[]{:S(2)}, u32[]{:S(2)}) %collective-permute-start.23) | collective-permute-done | bytes 393248 | tf_op jit(solution)/shard_map/cond/branch_1_fun/ppermute | solution.py:562
  83.6 2.3 %branch_1_fun.20 = (bf16[48,4096]{1,0:T(8,128)(2,1)S(1)}, bf16[48,4096]{1,0:T(8,128)(2,1)S(1)}) custom-call(bf16[2,512,512]{2,1,0:T(8,128)(2,1)S(1)} %get-tuple-element.273.lhs_ref, bf16[2,512,512]{2,1,0:T(8,128)(2,1)S(1)} %get-tuple-element.274.forward_ref, bf16[512,4096]{1,0:T(8,128)(2,1)S(1)} %get-tuple-element.259.up_ref, ...), custom_call_target="tpu_custom_call" | custom-call | bytes 10485760 | tf_op jit(solution)/shard_map/cond/branch_1_fun/pallas_call | solution.py:466
  85.9 4.0 %collective-permute-start.28 = (bf16[48,4096]{1,0:T(8,128)(2,1)S(1)}, bf16[48,4096]{1,0:T(8,128)(2,1)S(1)}, u32[]{:S(2)}, u32[]{:S(2)}) collective-permute-start(bf16[48,4096]{1,0:T(8,128)(2,1)S(1)} %get-tuple-element.285), channel_id=1, source_target_pairs={{0,4},{4,0},{8,12},{12,8},{1,5},{5,1},{9,13},{13,9},{2,6},{6,2},{1... | collective-permute-start | bytes 1179656 | tf_op jit(solution)/shard_map/cond/branch_1_fun/ppermute | solution.py:562
  89.9 0.7 collective-permute-start.29
  90.5 1.5 %collective-permute-done.25.refs_5_ = bf16[48,4096]{1,0:T(8,128)(2,1)S(1)} collective-permute-done((bf16[48,4096]{1,0:T(8,128)(2,1)S(1)}, bf16[48,4096]{1,0:T(8,128)(2,1)S(1)}, u32[]{:S(2)}, u32[]{:S(2)}) %collective-permute-start.25) | collective-permute-done | bytes 393248 | tf_op jit(solution)/shard_map/cond/branch_1_fun/ppermute | solution.py:562
  92.0 4.6 %branch_1_fun.19.early_ref = bf16[2,128,4096]{2,1,0:T(8,128)(2,1)S(1)} custom-call(bf16[2,256,512]{2,1,0:T(8,128)(2,1)S(1)} %get-tuple-element.247.arrive_ref, bf16[256,512]{1,0:T(8,128)(2,1)S(1)} %get-tuple-element.271.local_ref, bf16[512,4096]{1,0:T(8,128)(2,1)S(1)} %get-tuple-element.259.up_ref, bf16[48,4096]{1,0:T(8,128)(2,1)S(1)} %collective-permute-done.17.refs_0_, ...), custom_call_target="tpu_custom_call" | custom-call | bytes 1048576 | tf_op jit(solution)/shard_map/cond/branch_1_fun/pallas_call | solution.py:466
  96.6 3.4 %collective-permute-done.28.outer_ref = bf16[48,4096]{1,0:T(8,128)(2,1)S(1)} collective-permute-done((bf16[48,4096]{1,0:T(8,128)(2,1)S(1)}, bf16[48,4096]{1,0:T(8,128)(2,1)S(1)}, u32[]{:S(2)}, u32[]{:S(2)}) %collective-permute-start.28) | collective-permute-done | bytes 393248 | tf_op jit(solution)/shard_map/cond/branch_1_fun/ppermute | solution.py:562
  100.0 3.2 %branch_1_fun.21 = bf16[64,2,4096]{2,1,0:T(2,128)(2,1)S(1)} custom-call(s32[1]{0:T(128)} %bitcast.3.group_ref, bf16[2,256,512]{2,1,0:T(8,128)(2,1)S(1)} %get-tuple-element.247.arrive_ref, bf16[128,64]{1,0:T(8,128)(2,1)S(1)} %get-tuple-element.248.panel_ref, bf16[64,4096]{1,0:T(8,128)(2,1)S(1)} %branch_1_fun.12.mine_ref, ...), custom_call_target="tpu_custom_call" | custom-call | bytes 1048576 | tf_op jit(solution)/shard_map/cond/branch_1_fun/pallas_call | solution.py:466
  103.6 1.0 copy-done.6
  104.6 0.9 copy-done.1
  (44 shorter events, 4.0 us)
Async XLA Ops:
  0.0 1.5 %copy-start = (bf16[16,2,4096]{2,1,0:T(2,128)(2,1)S(1)}, bf16[16,2,4096]{2,1,0:T(2,128)(2,1)}, u32[]{:S(2)}) copy-start(bf16[16,2,4096]{2,1,0:T(2,128)(2,1)} %param.16) | copy-start | bytes 786436
  0.0 5.0 %collective-permute-start.89 = (s32[2,32,2]{1,2,0:T(2,128)}, s32[2,32,2]{1,2,0:T(2,128)S(1)}, u32[]{:S(2)}, u32[]{:S(2)}) collective-permute-start(s32[2,32,2]{1,2,0:T(2,128)} %param.13), channel_id=1, source_target_pairs={{0,0},{1,5},{2,10},{3,15},{4,4},{5,9},{6,14},{7,3},{8,8},{9,13},{1... | collective-permute-start | bytes 1544 | tf_op jit(solution)/shard_map/ppermute | solution.py:613
  1.9 23.8 %collective-permute-start.96 = (bf16[16,4096]{1,0:T(8,128)(2,1)S(1)}, bf16[16,4096]{1,0:T(8,128)(2,1)S(1)}, u32[]{:S(2)}, u32[]{:S(2)}) collective-permute-start(bf16[16,4096]{1,0:T(8,128)(2,1)S(1)} %bitcast.35), channel_id=1, source_target_pairs={{0,4},{4,0},{8,12},{12,8},{1,5},{5,1},{9,13},{13,9},{2,6},{6,2},{1... | collective-permute-start | bytes 393224 | tf_op jit(solution)/shard_map/ppermute | solution.py:479
  5.0 20.7 %collective-permute-start.93 = (bf16[64,1536]{1,0:T(8,128)(2,1)}, bf16[64,1536]{1,0:T(8,128)(2,1)S(1)}, u32[]{:S(2)}, u32[]{:S(2)}) collective-permute-start(bf16[64,1536]{1,0:T(8,128)(2,1)} %bitcast.26), channel_id=1, source_target_pairs={{0,4},{4,8},{8,12},{12,0},{1,5},{5,9},{9,13},{13,1},{2,6},{6,10},{... | collective-permute-start | bytes 589832 | tf_op jit(solution)/shard_map/ppermute | solution.py:607
  5.1 20.6 %collective-permute-start.94 = (bf16[64,1536]{1,0:T(8,128)(2,1)}, bf16[64,1536]{1,0:T(8,128)(2,1)S(1)}, u32[]{:S(2)}, u32[]{:S(2)}) collective-permute-start(bf16[64,1536]{1,0:T(8,128)(2,1)} %bitcast.27), channel_id=1, source_target_pairs={{0,8},{4,12},{8,0},{12,4},{1,9},{5,13},{9,1},{13,5},{2,10},{6,14},... | collective-permute-start | bytes 589832 | tf_op jit(solution)/shard_map/ppermute | solution.py:607
  8.1 17.7 %collective-permute-start.95 = (bf16[64,1536]{1,0:T(8,128)(2,1)}, bf16[64,1536]{1,0:T(8,128)(2,1)S(1)}, u32[]{:S(2)}, u32[]{:S(2)}) collective-permute-start(bf16[64,1536]{1,0:T(8,128)(2,1)} %bitcast.28), channel_id=1, source_target_pairs={{0,12},{4,0},{8,4},{12,8},{1,13},{5,1},{9,5},{13,9},{2,14},{6,2},{... | collective-permute-start | bytes 589832 | tf_op jit(solution)/shard_map/ppermute | solution.py:607
  10.7 1.5 %collective-permute-start.90 = (bf16[16,128]{1,0:T(8,128)(2,1)S(1)}, bf16[16,128]{1,0:T(8,128)(2,1)S(1)}, u32[]{:S(2)}, u32[]{:S(2)}) collective-permute-start(bf16[16,128]{1,0:T(8,128)(2,1)S(1)} %fusion.2.refs_0_), channel_id=1, source_target_pairs={{0,1},{1,0},{2,3},{3,2},{4,5},{5,4},{6,7},{7,6},{8,9},{9,8},{10,11... | collective-permute-start | bytes 12296 | tf_op jit(solution)/shard_map/ppermute | solution.py:618
  12.2 6.0 %collective-permute-start.91 = (bf16[32,128]{1,0:T(8,128)(2,1)S(1)}, bf16[32,128]{1,0:T(8,128)(2,1)S(1)}, u32[]{:S(2)}, u32[]{:S(2)}) collective-permute-start(bf16[32,128]{1,0:T(8,128)(2,1)S(1)} %pad_maximum_fusion), channel_id=1, source_target_pairs={{0,2},{2,0},{1,3},{3,1},{4,6},{6,4},{5,7},{7,5},{8,10},{10,8},{9,1... | collective-permute-start | bytes 24584 | tf_op jit(solution)/shard_map/ppermute | solution.py:619
  19.4 5.6 %collective-permute-start.92 = (f32[8,128]{1,0:T(8,128)S(1)}, f32[8,128]{1,0:T(8,128)S(1)}, u32[]{:S(2)}, u32[]{:S(2)}) collective-permute-start(f32[8,128]{1,0:T(8,128)S(1)} %get-tuple-element.474.own_ref), channel_id=1, source_target_pairs={{0,16},{16,0},{1,17},{17,1},{2,18},{18,2},{3,19},{19,3},{4,20},{20... | collective-permute-start | bytes 12296 | tf_op jit(solution)/shard_map/ppermute | solution.py:507
  21.0 2.2 %copy-start.2 = (bf16[16,2,16,4096]{3,2,1,0:T(8,128)(2,1)S(1)}, bf16[16,2,16,4096]{3,2,1,0:T(8,128)(2,1)}, u32[]{:S(2)}) copy-start(bf16[16,2,16,4096]{3,2,1,0:T(8,128)(2,1)} %param.15) | copy-start | bytes 12582916
  23.2 1.4 %copy-start.3 = (bf16[16,2,16,1536]{3,2,1,0:T(8,128)(2,1)S(1)}, bf16[16,2,16,1536]{3,2,1,0:T(8,128)(2,1)}, u32[]{:S(2)}) copy-start(bf16[16,2,16,1536]{3,2,1,0:T(8,128)(2,1)} %down_ref) | copy-start | bytes 4718596
  24.6 1.1 %copy-start.4 = (bf16[2,32,1536]{2,1,0:T(8,128)(2,1)S(1)}, bf16[2,32,1536]{2,1,0:T(8,128)(2,1)}, u32[]{:S(2)}) copy-start(bf16[2,32,1536]{2,1,0:T(8,128)(2,1)} %param.11) | copy-start | bytes 589828
  26.5 8.5 %collective-permute-start.100 = (bf16[32,4096]{1,0:T(8,128)(2,1)S(1)}, bf16[32,4096]{1,0:T(8,128)(2,1)S(1)}, u32[]{:S(2)}, u32[]{:S(2)}) collective-permute-start(bf16[32,4096]{1,0:T(8,128)(2,1)S(1)} %get-tuple-element.488), channel_id=1, source_target_pairs={{4,8},{8,4},{5,9},{9,5},{6,10},{10,6},{7,11},{11,7},{20,24},{24,20... | collective-permute-start | bytes 786440 | tf_op jit(solution)/shard_map/ppermute | solution.py:521
  27.2 2.8 %collective-permute-start.97 = (f32[32,512]{1,0:T(8,128)S(1)}, f32[32,512]{1,0:T(8,128)S(1)}, u32[]{:S(2)}, u32[]{:S(2)}) collective-permute-start(f32[32,512]{1,0:T(8,128)S(1)} %get-tuple-element.486.own_ref), channel_id=1, source_target_pairs={{0,1},{1,0},{2,3},{3,2},{4,5},{5,4},{6,7},{7,6},{8,9},{9,8},{10,11... | collective-permute-start | bytes 196616 | tf_op jit(solution)/shard_map/ppermute | solution.py:520
  27.2 4.8 %collective-permute-start.98 = (f32[32,512]{1,0:T(8,128)S(1)}, f32[32,512]{1,0:T(8,128)S(1)}, u32[]{:S(2)}, u32[]{:S(2)}) collective-permute-start(f32[32,512]{1,0:T(8,128)S(1)} %get-tuple-element.486.own_ref), channel_id=1, source_target_pairs={{0,2},{1,3},{2,0},{3,1},{4,6},{5,7},{6,4},{7,5},{8,10},{9,11},{10,... | collective-permute-start | bytes 196616 | tf_op jit(solution)/shard_map/ppermute | solution.py:520
  29.3 4.0 %collective-permute-start.99 = (f32[32,512]{1,0:T(8,128)S(1)}, f32[32,512]{1,0:T(8,128)S(1)}, u32[]{:S(2)}, u32[]{:S(2)}) collective-permute-start(f32[32,512]{1,0:T(8,128)S(1)} %get-tuple-element.486.own_ref), channel_id=1, source_target_pairs={{0,3},{1,2},{2,1},{3,0},{4,7},{5,6},{6,5},{7,4},{8,11},{9,10},{10,... | collective-permute-start | bytes 196616 | tf_op jit(solution)/shard_map/ppermute | solution.py:520
  33.4 1.6 %copy-start.5 = (bf16[2,32,2,2,4096]{4,3,2,1,0:T(2,128)(2,1)S(1)}, bf16[2,32,2,2,4096]{4,3,2,1,0:T(2,128)(2,1)}, u32[]{:S(2)}) copy-start(bf16[2,32,2,2,4096]{4,3,2,1,0:T(2,128)(2,1)} %param.12) | copy-start | bytes 6291460
  35.0 16.6 %collective-permute-start.17 = (bf16[48,4096]{1,0:T(8,128)(2,1)S(1)}, bf16[48,4096]{1,0:T(8,128)(2,1)S(1)}, u32[]{:S(2)}, u32[]{:S(2)}) collective-permute-start(bf16[48,4096]{1,0:T(8,128)(2,1)S(1)} %get-tuple-element.272), channel_id=1, source_target_pairs={{0,4},{4,0},{8,12},{12,8},{1,5},{5,1},{9,13},{13,9},{2,6},{6,2},{1... | collective-permute-start | bytes 1179656 | tf_op jit(solution)/shard_map/cond/branch_1_fun/ppermute | solution.py:562
  40.0 11.6 %collective-permute-start.18 = (bf16[48,4096]{1,0:T(8,128)(2,1)S(1)}, bf16[48,4096]{1,0:T(8,128)(2,1)S(1)}, u32[]{:S(2)}, u32[]{:S(2)}) collective-permute-start(bf16[48,4096]{1,0:T(8,128)(2,1)S(1)} %get-tuple-element.275), channel_id=1, source_target_pairs={{4,8},{8,4},{5,9},{9,5},{6,10},{10,6},{7,11},{11,7},{20,24},{24,20... | collective-permute-start | bytes 1179656 | tf_op jit(solution)/shard_map/cond/branch_1_fun/ppermute | solution.py:561
  42.2 16.1 %collective-permute-start.15 = (bf16[48,4096]{1,0:T(8,128)(2,1)S(1)}, bf16[48,4096]{1,0:T(8,128)(2,1)S(1)}, u32[]{:S(2)}, u32[]{:S(2)}) collective-permute-start(bf16[48,4096]{1,0:T(8,128)(2,1)S(1)} %get-tuple-element.260), channel_id=1, source_target_pairs={{0,4},{4,0},{8,12},{12,8},{1,5},{5,1},{9,13},{13,9},{2,6},{6,2},{1... | collective-permute-start | bytes 1179656 | tf_op jit(solution)/shard_map/cond/branch_1_fun/ppermute | solution.py:562
  45.6 12.7 %collective-permute-start.20 = (bf16[48,4096]{1,0:T(8,128)(2,1)S(1)}, bf16[48,4096]{1,0:T(8,128)(2,1)S(1)}, u32[]{:S(2)}, u32[]{:S(2)}) collective-permute-start(bf16[48,4096]{1,0:T(8,128)(2,1)S(1)} %get-tuple-element.277), channel_id=1, source_target_pairs={{4,8},{8,4},{5,9},{9,5},{6,10},{10,6},{7,11},{11,7},{20,24},{24,20... | collective-permute-start | bytes 1179656 | tf_op jit(solution)/shard_map/cond/branch_1_fun/ppermute | solution.py:561
  53.6 13.1 %collective-permute-start.19 = (bf16[48,4096]{1,0:T(8,128)(2,1)S(1)}, bf16[48,4096]{1,0:T(8,128)(2,1)S(1)}, u32[]{:S(2)}, u32[]{:S(2)}) collective-permute-start(bf16[48,4096]{1,0:T(8,128)(2,1)S(1)} %get-tuple-element.276), channel_id=1, source_target_pairs={{0,4},{4,0},{8,12},{12,8},{1,5},{5,1},{9,13},{13,9},{2,6},{6,2},{1... | collective-permute-start | bytes 1179656 | tf_op jit(solution)/shard_map/cond/branch_1_fun/ppermute | solution.py:562
  55.9 10.8 %collective-permute-start.22 = (bf16[48,4096]{1,0:T(8,128)(2,1)S(1)}, bf16[48,4096]{1,0:T(8,128)(2,1)S(1)}, u32[]{:S(2)}, u32[]{:S(2)}) collective-permute-start(bf16[48,4096]{1,0:T(8,128)(2,1)S(1)} %get-tuple-element.279), channel_id=1, source_target_pairs={{4,8},{8,4},{5,9},{9,5},{6,10},{10,6},{7,11},{11,7},{20,24},{24,20... | collective-permute-start | bytes 1179656 | tf_op jit(solution)/shard_map/cond/branch_1_fun/ppermute | solution.py:561
  60.3 14.8 %collective-permute-start.21 = (bf16[48,4096]{1,0:T(8,128)(2,1)S(1)}, bf16[48,4096]{1,0:T(8,128)(2,1)S(1)}, u32[]{:S(2)}, u32[]{:S(2)}) collective-permute-start(bf16[48,4096]{1,0:T(8,128)(2,1)S(1)} %get-tuple-element.278), channel_id=1, source_target_pairs={{0,4},{4,0},{8,12},{12,8},{1,5},{5,1},{9,13},{13,9},{2,6},{6,2},{1... | collective-permute-start | bytes 1179656 | tf_op jit(solution)/shard_map/cond/branch_1_fun/ppermute | solution.py:562
  64.3 10.8 %collective-permute-start.24 = (bf16[48,4096]{1,0:T(8,128)(2,1)S(1)}, bf16[48,4096]{1,0:T(8,128)(2,1)S(1)}, u32[]{:S(2)}, u32[]{:S(2)}) collective-permute-start(bf16[48,4096]{1,0:T(8,128)(2,1)S(1)} %get-tuple-element.281), channel_id=1, source_target_pairs={{4,8},{8,4},{5,9},{9,5},{6,10},{10,6},{7,11},{11,7},{20,24},{24,20... | collective-permute-start | bytes 1179656 | tf_op jit(solution)/shard_map/cond/branch_1_fun/ppermute | solution.py:561
  68.8 14.8 %collective-permute-start.23 = (bf16[48,4096]{1,0:T(8,128)(2,1)S(1)}, bf16[48,4096]{1,0:T(8,128)(2,1)S(1)}, u32[]{:S(2)}, u32[]{:S(2)}) collective-permute-start(bf16[48,4096]{1,0:T(8,128)(2,1)S(1)} %get-tuple-element.280), channel_id=1, source_target_pairs={{0,4},{4,0},{8,12},{12,8},{1,5},{5,1},{9,13},{13,9},{2,6},{6,2},{1... | collective-permute-start | bytes 1179656 | tf_op jit(solution)/shard_map/cond/branch_1_fun/ppermute | solution.py:562
  72.8 10.8 %collective-permute-start.26 = (bf16[48,4096]{1,0:T(8,128)(2,1)S(1)}, bf16[48,4096]{1,0:T(8,128)(2,1)S(1)}, u32[]{:S(2)}, u32[]{:S(2)}) collective-permute-start(bf16[48,4096]{1,0:T(8,128)(2,1)S(1)} %get-tuple-element.283), channel_id=1, source_target_pairs={{4,8},{8,4},{5,9},{9,5},{6,10},{10,6},{7,11},{11,7},{20,24},{24,20... | collective-permute-start | bytes 1179656 | tf_op jit(solution)/shard_map/cond/branch_1_fun/ppermute | solution.py:561
  73.5 26.5 %collective-permute-start.16 = (bf16[64,4096]{1,0:T(8,128)(2,1)S(1)}, bf16[64,4096]{1,0:T(8,128)(2,1)S(1)}, u32[]{:S(2)}, u32[]{:S(2)}) collective-permute-start(bf16[64,4096]{1,0:T(8,128)(2,1)S(1)} %branch_1_fun.12.mine_ref), channel_id=1, source_target_pairs={{0,16},{16,0},{1,17},{17,1},{2,18},{18,2},{3,19},{19,3},{4,20},{20... | collective-permute-start | bytes 1572872 | tf_op jit(solution)/shard_map/cond/branch_1_fun/ppermute | solution.py:569
  77.3 14.7 %collective-permute-start.25 = (bf16[48,4096]{1,0:T(8,128)(2,1)S(1)}, bf16[48,4096]{1,0:T(8,128)(2,1)S(1)}, u32[]{:S(2)}, u32[]{:S(2)}) collective-permute-start(bf16[48,4096]{1,0:T(8,128)(2,1)S(1)} %get-tuple-element.282), channel_id=1, source_target_pairs={{0,4},{4,0},{8,12},{12,8},{1,5},{5,1},{9,13},{13,9},{2,6},{6,2},{1... | collective-permute-start | bytes 1179656 | tf_op jit(solution)/shard_map/cond/branch_1_fun/ppermute | solution.py:562
  81.3 10.7 %collective-permute-start.27 = (bf16[48,4096]{1,0:T(8,128)(2,1)S(1)}, bf16[48,4096]{1,0:T(8,128)(2,1)S(1)}, u32[]{:S(2)}, u32[]{:S(2)}) collective-permute-start(bf16[48,4096]{1,0:T(8,128)(2,1)S(1)} %get-tuple-element.284), channel_id=1, source_target_pairs={{4,8},{8,4},{5,9},{9,5},{6,10},{10,6},{7,11},{11,7},{20,24},{24,20... | collective-permute-start | bytes 1179656 | tf_op jit(solution)/shard_map/cond/branch_1_fun/ppermute | solution.py:561
  85.9 14.1 %collective-permute-start.28 = (bf16[48,4096]{1,0:T(8,128)(2,1)S(1)}, bf16[48,4096]{1,0:T(8,128)(2,1)S(1)}, u32[]{:S(2)}, u32[]{:S(2)}) collective-permute-start(bf16[48,4096]{1,0:T(8,128)(2,1)S(1)} %get-tuple-element.285), channel_id=1, source_target_pairs={{0,4},{4,0},{8,12},{12,8},{1,5},{5,1},{9,13},{13,9},{2,6},{6,2},{1... | collective-permute-start | bytes 1179656 | tf_op jit(solution)/shard_map/cond/branch_1_fun/ppermute | solution.py:562
  89.9 10.1 %collective-permute-start.29 = (bf16[48,4096]{1,0:T(8,128)(2,1)S(1)}, bf16[48,4096]{1,0:T(8,128)(2,1)S(1)}, u32[]{:S(2)}, u32[]{:S(2)}) collective-permute-start(bf16[48,4096]{1,0:T(8,128)(2,1)S(1)} %get-tuple-element.286), channel_id=1, source_target_pairs={{4,8},{8,4},{5,9},{9,5},{6,10},{10,6},{7,11},{11,7},{20,24},{24,20... | collective-permute-start | bytes 1179656 | tf_op jit(solution)/shard_map/cond/branch_1_fun/ppermute | solution.py:561
  103.6 1.0 copy-start.6
  104.6 0.9 copy-start.1

commit v2 on v1

--- a/solution.py
+++ b/solution.py
@@ -414,15 +414,13 @@
         pick_ref[:, way * size : (way + 1) * size] = nt_dot(arrive_ref[way], last).astype(jnp.bfloat16)
 
     def body(cols):
-        scales = [
-            jnp.dot(panel_ref[...], ref[:, cols], preferred_element_type=jnp.float32) for ref in (mine_ref, other_ref)
-        ]
         late = jnp.concatenate([outer_ref[:, cols], middle_ref[:, cols]], axis=0)
         picked = jnp.dot(pick_ref[...], late, preferred_element_type=jnp.float32)
         adapted = []
         for p in range(2):
             delta = early_ref[p, :, cols].astype(jnp.float32) + picked[p * routes : (p + 1) * routes]
-            scale = jnp.where(group == p, scales[0], scales[1])
+            scales = jnp.where(group == p, mine_ref[:, cols], other_ref[:, cols])
+            scale = jnp.dot(panel_ref[...], scales, preferred_element_type=jnp.float32)
             adapted.append(scale * (base_ref[p, :, cols].astype(jnp.float32) + delta))
         gate, value = adapted
         hidden = (gate / (1.0 + jnp.exp(-gate)) * value).astype(out_ref.dtype)

time: 107 us -> 106 us (level)
  waiting for transfers between devices: 15.8 us -> 17.6 us
  starting transfers between devices: 52.4 us -> 50.6 us
    ppermute x7, starting transfers between devices: 26.6 us -> 24.7 us  [flow(): got_outer.append(lax.ppermute(outer, 'dp', outer_pairs))]
    ppermute x7, waiting for transfers between devices: 9.89 us -> 11.7 us  [flow(): got_outer.append(lax.ppermute(outer, 'dp', outer_pairs))]
  transfers between devices with their start and end apart: 27 -> 27, of which waited for: 9 -> 8; matrix products, arithmetic and copies ran while one was open for 1% -> 1% of each run, Pallas kernels for 25% -> 25%
where the time goes in v2:
time: 106 us; the launch traced here: 105 us
  starting transfers between devices  50.6 us (48%)
  Pallas kernels  29.6 us (28%)
  waiting for transfers between devices  17.6 us (17%)
  local copies, waits for them, and re-layouts  6.07 us (6%)
    pallas_call x16, Pallas kernels, kernel(): pl.pallas_call(body, out_shape=[jax.ShapeDtypeStruct(shape, dtype) for sh...  29.6 us
    ppermute x7, starting transfers between devices, flow(): got_outer.append(lax.ppermute(outer, 'dp', outer_pairs))  24.7 us
    ppermute x7, waiting for transfers between devices, flow(): got_outer.append(lax.ppermute(outer, 'dp', outer_pairs))  11.7 us
    unnamed x15, local copies, waits for them, and re-layouts  5.68 us
    ppermute x3, starting transfers between devices, turn(): lax.ppermute(x, 'dp', [(i, (i + shift) % count) for i in range(count)])  5.51 us
    ppermute x7, starting transfers between devices, flow(): got_middle.append(lax.ppermute(middle, 'dp', middle_pair))  4.72 us
    ppermute x1, starting transfers between devices, on_device(): lax.ppermute(jnp.concatenate([near, beside], axis=0), 'expert', [(0, 1),...  4.33 us
    ppermute x3, waiting for transfers between devices, relayed(): lax.ppermute(part, ('expert', 'pair'), [(i, i ^ mask) for i in range(4)])  3.4 us
  transfers between devices with their start and end apart: 27, of which 8 were waited for; matrix products, arithmetic and copies ran while one was open for 1% of the time, Pallas kernels for 25%

profile of v2, /device:TPU:0, one launch (start us, length us, event | category | flops | bytes accessed | tf_op | source)
XLA Modules:
  0.0 105.2 jit_solution(16717009547639638042)
XLA Ops:
  0.0 1.5 %collective-permute-start.89 = (s32[2,32,2]{1,2,0:T(2,128)}, s32[2,32,2]{1,2,0:T(2,128)S(1)}, u32[]{:S(2)}, u32[]{:S(2)}) collective-permute-start(s32[2,32,2]{1,2,0:T(2,128)} %param.13), channel_id=1, source_target_pairs={{0,0},{1,5},{2,10},{3,15},{4,4},{5,9},{6,14},{7,3},{8,8},{9,13},{1... | collective-permute-start | bytes 1544 | tf_op jit(solution)/shard_map/ppermute | solution.py:611
  1.9 3.1 %collective-permute-start.96 = (bf16[16,4096]{1,0:T(8,128)(2,1)S(1)}, bf16[16,4096]{1,0:T(8,128)(2,1)S(1)}, u32[]{:S(2)}, u32[]{:S(2)}) collective-permute-start(bf16[16,4096]{1,0:T(8,128)(2,1)S(1)} %bitcast.35), channel_id=1, source_target_pairs={{0,4},{4,0},{8,12},{12,8},{1,5},{5,1},{9,13},{13,9},{2,6},{6,2},{1... | collective-permute-start | bytes 393224 | tf_op jit(solution)/shard_map/ppermute | solution.py:477
  5.1 3.0 %collective-permute-start.94 = (bf16[64,1536]{1,0:T(8,128)(2,1)}, bf16[64,1536]{1,0:T(8,128)(2,1)S(1)}, u32[]{:S(2)}, u32[]{:S(2)}) collective-permute-start(bf16[64,1536]{1,0:T(8,128)(2,1)} %bitcast.27), channel_id=1, source_target_pairs={{0,8},{4,12},{8,0},{12,4},{1,9},{5,13},{9,1},{13,5},{2,10},{6,14},... | collective-permute-start | bytes 589832 | tf_op jit(solution)/shard_map/ppermute | solution.py:605
  8.1 2.5 %collective-permute-start.95 = (bf16[64,1536]{1,0:T(8,128)(2,1)}, bf16[64,1536]{1,0:T(8,128)(2,1)S(1)}, u32[]{:S(2)}, u32[]{:S(2)}) collective-permute-start(bf16[64,1536]{1,0:T(8,128)(2,1)} %bitcast.28), channel_id=1, source_target_pairs={{0,12},{4,0},{8,4},{12,8},{1,13},{5,1},{9,5},{13,9},{2,14},{6,2},{... | collective-permute-start | bytes 589832 | tf_op jit(solution)/shard_map/ppermute | solution.py:605
  10.7 0.7 collective-permute-start.90
  11.4 0.8 collective-permute-done.90.refs_1_
  12.2 4.3 %collective-permute-start.91 = (bf16[32,128]{1,0:T(8,128)(2,1)S(1)}, bf16[32,128]{1,0:T(8,128)(2,1)S(1)}, u32[]{:S(2)}, u32[]{:S(2)}) collective-permute-start(bf16[32,128]{1,0:T(8,128)(2,1)S(1)} %pad_maximum_fusion), channel_id=1, source_target_pairs={{0,2},{2,0},{1,3},{3,1},{4,6},{6,4},{5,7},{7,5},{8,10},{10,8},{9,1... | collective-permute-start | bytes 24584 | tf_op jit(solution)/shard_map/ppermute | solution.py:617
  16.5 1.6 %collective-permute-done.91.refs_2_ = bf16[32,128]{1,0:T(8,128)(2,1)S(1)} collective-permute-done((bf16[32,128]{1,0:T(8,128)(2,1)S(1)}, bf16[32,128]{1,0:T(8,128)(2,1)S(1)}, u32[]{:S(2)}, u32[]{:S(2)}) %collective-permute-start.91) | collective-permute-done | bytes 8224 | tf_op jit(solution)/shard_map/ppermute | solution.py:617
  18.1 1.3 %shard_map.69 = (f32[16,512]{1,0:T(8,128)S(1)}, f32[8,128]{1,0:T(8,128)S(1)}, bf16[2,512,512]{2,1,0:T(8,128)(2,1)S(1)}, bf16[192,512]{1,0:T(8,128)(2,1)S(1)}, bf...) custom-call(s32[1]{0:T(128)} %bitcast.15.me_ref, s32[1]{0:T(128)} %bitcast.16.part_ref, ...), custom_call_target="tpu_custom_call" | custom-call | bytes 134217728 | tf_op jit(solution)/shard_map/pallas_call | solution.py:464
  19.4 1.6 %collective-permute-start.92 = (f32[8,128]{1,0:T(8,128)S(1)}, f32[8,128]{1,0:T(8,128)S(1)}, u32[]{:S(2)}, u32[]{:S(2)}) collective-permute-start(f32[8,128]{1,0:T(8,128)S(1)} %get-tuple-element.474.own_ref), channel_id=1, source_target_pairs={{0,16},{16,0},{1,17},{17,1},{2,18},{18,2},{3,19},{19,3},{4,20},{20... | collective-permute-start | bytes 12296 | tf_op jit(solution)/shard_map/ppermute | solution.py:505
  21.0 2.2 %copy-done.2 = bf16[16,2,16,4096]{3,2,1,0:T(8,128)(2,1)S(1)} copy-done((bf16[16,2,16,4096]{3,2,1,0:T(8,128)(2,1)S(1)}, bf16[16,2,16,4096]{3,2,1,0:T(8,128)(2,1)}, u32[]{:S(2)}) %copy-start.2) | copy-done | bytes 4194328
  23.2 1.4 %copy-done.3 = bf16[16,2,16,1536]{3,2,1,0:T(8,128)(2,1)S(1)} copy-done((bf16[16,2,16,1536]{3,2,1,0:T(8,128)(2,1)S(1)}, bf16[16,2,16,1536]{3,2,1,0:T(8,128)(2,1)}, u32[]{:S(2)}) %copy-start.3) | copy-done | bytes 1572888
  25.8 0.7 shard_map.72
  26.5 0.7 collective-permute-start.100
  27.2 2.1 %collective-permute-start.98 = (f32[32,512]{1,0:T(8,128)S(1)}, f32[32,512]{1,0:T(8,128)S(1)}, u32[]{:S(2)}, u32[]{:S(2)}) collective-permute-start(f32[32,512]{1,0:T(8,128)S(1)} %get-tuple-element.486.own_ref), channel_id=1, source_target_pairs={{0,2},{1,3},{2,0},{3,1},{4,6},{5,7},{6,4},{7,5},{8,10},{9,11},{10,... | collective-permute-start | bytes 196616 | tf_op jit(solution)/shard_map/ppermute | solution.py:518
  30.0 2.0 %collective-permute-done.98.far_ref = f32[32,512]{1,0:T(8,128)S(1)} collective-permute-done((f32[32,512]{1,0:T(8,128)S(1)}, f32[32,512]{1,0:T(8,128)S(1)}, u32[]{:S(2)}, u32[]{:S(2)}) %collective-permute-start.98) | collective-permute-done | bytes 65568 | tf_op jit(solution)/shard_map/ppermute | solution.py:518
  32.0 1.4 %collective-permute-done.99.diag_ref = f32[32,512]{1,0:T(8,128)S(1)} collective-permute-done((f32[32,512]{1,0:T(8,128)S(1)}, f32[32,512]{1,0:T(8,128)S(1)}, u32[]{:S(2)}, u32[]{:S(2)}) %collective-permute-start.99) | collective-permute-done | bytes 65568 | tf_op jit(solution)/shard_map/ppermute | solution.py:518
  33.4 1.6 %shard_map.73 = (bf16[48,4096]{1,0:T(8,128)(2,1)S(1)}, bf16[48,4096]{1,0:T(8,128)(2,1)S(1)}) custom-call(bf16[192,512]{1,0:T(8,128)(2,1)S(1)} %get-tuple-element.477.first_ref, bf16[192,512]{1,0:T(8,128)(2,1)S(1)} %get-tuple-element.478.held_ref, f32[32,512]{1,0:T(8,128)S(1)} %get-tuple-element.486.own_ref, f32[32,512]{1,0:T(8,128)S(1)} %collective-permute-done.97.core_ref, ...), custom_call_target="tpu_custom_call" | custom-call | bytes 1048576 | tf_op jit(solution)/shard_map/pallas_call | solution.py:464
  35.0 68.3 %conditional.1 = (bf16[2,32,2,4096]{3,2,1,0:T(2,128)(2,1)S(1)}) conditional(s32[]{:T(128)} %bitcast.21, (s32[]{:T(128)}, s32[]{:T(128)}, bf16[192,512]{1,0:T(8,128)(2,1)S(1)}, bf16[192,512]{1,0:T(8,128)(2,1)S(1)}, f32[32,512]{1,0:T(8,128)S(1)}, /*index=5*/f32[32,512]{1,0:T(8,128)S(1)}, f32[32,512]{1,0:T(8,128)S(1)}, ...), branch_computations={%region_0.1_spmd, %region_1.2_spmd, %region_2.3_spmd, %region_3.4_... | conditional | bytes 136315808 | solution.py:588
  35.0 5.0 %collective-permute-start.2 = (bf16[48,4096]{1,0:T(8,128)(2,1)S(1)}, bf16[48,4096]{1,0:T(8,128)(2,1)S(1)}, u32[]{:S(2)}, u32[]{:S(2)}) collective-permute-start(bf16[48,4096]{1,0:T(8,128)(2,1)S(1)} %get-tuple-element.228), channel_id=1, source_target_pairs={{0,4},{4,0},{8,12},{12,8},{1,5},{5,1},{9,13},{13,9},{2,6},{6,2},{1... | collective-permute-start | bytes 1179656 | tf_op jit(solution)/shard_map/cond/branch_0_fun/ppermute | solution.py:560
  40.0 0.7 collective-permute-start.3
  40.7 1.6 %branch_0_fun.11 = (bf16[48,4096]{1,0:T(8,128)(2,1)S(1)}, bf16[48,4096]{1,0:T(8,128)(2,1)S(1)}) custom-call(bf16[192,512]{1,0:T(8,128)(2,1)S(1)} %get-tuple-element.209.first_ref, bf16[192,512]{1,0:T(8,128)(2,1)S(1)} %get-tuple-element.210.held_ref, f32[32,512]{1,0:T(8,128)S(1)} %get-tuple-element.223.own_ref, f32[32,512]{1,0:T(8,128)S(1)} %get-tuple-element.224.core_ref, ...), custom_call_target="tpu_custom_call" | custom-call | bytes 1048576 | tf_op jit(solution)/shard_map/cond/branch_0_fun/pallas_call | solution.py:464
  42.2 3.3 %collective-permute-start = (bf16[48,4096]{1,0:T(8,128)(2,1)S(1)}, bf16[48,4096]{1,0:T(8,128)(2,1)S(1)}, u32[]{:S(2)}, u32[]{:S(2)}) collective-permute-start(bf16[48,4096]{1,0:T(8,128)(2,1)S(1)} %get-tuple-element.216), channel_id=1, source_target_pairs={{0,4},{4,0},{8,12},{12,8},{1,5},{5,1},{9,13},{13,9},{2,6},{6,2},{1... | collective-permute-start | bytes 1179656 | tf_op jit(solution)/shard_map/cond/branch_0_fun/ppermute | solution.py:560
  45.6 0.7 collective-permute-start.5
  46.2 4.5 %branch_0_fun.13.base_ref = bf16[2,128,4096]{2,1,0:T(8,128)(2,1)S(1)} custom-call(bf16[64,2,2,4096]{3,2,1,0:T(2,128)(2,1)S(1)} %get-tuple-element.219.base_ref), custom_call_target="tpu_custom_call" | custom-call | bytes 1048576 | tf_op jit(solution)/shard_map/cond/branch_0_fun/pallas_call | solution.py:464
  50.7 0.8 branch_0_fun.14
  51.6 2.0 %branch_0_fun.15 = (bf16[48,4096]{1,0:T(8,128)(2,1)S(1)}, bf16[48,4096]{1,0:T(8,128)(2,1)S(1)}) custom-call(bf16[2,512,512]{2,1,0:T(8,128)(2,1)S(1)} %get-tuple-element.229.lhs_ref, bf16[2,512,512]{2,1,0:T(8,128)(2,1)S(1)} %get-tuple-element.230.forward_ref, bf16[512,4096]{1,0:T(8,128)(2,1)S(1)} %get-tuple-element.215.up_ref, ...), custom_call_target="tpu_custom_call" | custom-call | bytes 6291456 | tf_op jit(solution)/shard_map/cond/branch_0_fun/pallas_call | solution.py:464
  53.6 2.3 %collective-permute-start.4 = (bf16[48,4096]{1,0:T(8,128)(2,1)S(1)}, bf16[48,4096]{1,0:T(8,128)(2,1)S(1)}, u32[]{:S(2)}, u32[]{:S(2)}) collective-permute-start(bf16[48,4096]{1,0:T(8,128)(2,1)S(1)} %get-tuple-element.232), channel_id=1, source_target_pairs={{0,4},{4,0},{8,12},{12,8},{1,5},{5,1},{9,13},{13,9},{2,6},{6,2},{1... | collective-permute-start | bytes 1179656 | tf_op jit(solution)/shard_map/cond/branch_0_fun/ppermute | solution.py:560
  55.9 0.7 collective-permute-start.7
  56.6 1.7 %collective-permute-done.second_ref.refs_1_ = bf16[48,4096]{1,0:T(8,128)(2,1)S(1)} collective-permute-done((bf16[48,4096]{1,0:T(8,128)(2,1)S(1)}, bf16[48,4096]{1,0:T(8,128)(2,1)S(1)}, u32[]{:S(2)}, u32[]{:S(2)}) %collective-permute-start) | collective-permute-done | bytes 393248 | tf_op jit(solution)/shard_map/cond/branch_0_fun/ppermute | solution.py:560
  58.3 2.0 %branch_0_fun.16 = (bf16[48,4096]{1,0:T(8,128)(2,1)S(1)}, bf16[48,4096]{1,0:T(8,128)(2,1)S(1)}) custom-call(bf16[2,512,512]{2,1,0:T(8,128)(2,1)S(1)} %get-tuple-element.229.lhs_ref, bf16[2,512,512]{2,1,0:T(8,128)(2,1)S(1)} %get-tuple-element.230.forward_ref, bf16[512,4096]{1,0:T(8,128)(2,1)S(1)} %get-tuple-element.215.up_ref, ...), custom_call_target="tpu_custom_call" | custom-call | bytes 7340032 | tf_op jit(solution)/shard_map/cond/branch_0_fun/pallas_call | solution.py:464
  60.3 4.0 %collective-permute-start.6 = (bf16[48,4096]{1,0:T(8,128)(2,1)S(1)}, bf16[48,4096]{1,0:T(8,128)(2,1)S(1)}, u32[]{:S(2)}, u32[]{:S(2)}) collective-permute-start(bf16[48,4096]{1,0:T(8,128)(2,1)S(1)} %get-tuple-element.234), channel_id=1, source_target_pairs={{0,4},{4,0},{8,12},{12,8},{1,5},{5,1},{9,13},{13,9},{2,6},{6,2},{1... | collective-permute-start | bytes 1179656 | tf_op jit(solution)/shard_map/cond/branch_0_fun/ppermute | solution.py:560
  64.3 0.7 collective-permute-start.9
  65.0 1.7 %collective-permute-done.4.refs_2_ = bf16[48,4096]{1,0:T(8,128)(2,1)S(1)} collective-permute-done((bf16[48,4096]{1,0:T(8,128)(2,1)S(1)}, bf16[48,4096]{1,0:T(8,128)(2,1)S(1)}, u32[]{:S(2)}, u32[]{:S(2)}) %collective-permute-start.4) | collective-permute-done | bytes 393248 | tf_op jit(solution)/shard_map/cond/branch_0_fun/ppermute | solution.py:560
  66.7 2.1 %branch_0_fun.17 = (bf16[48,4096]{1,0:T(8,128)(2,1)S(1)}, bf16[48,4096]{1,0:T(8,128)(2,1)S(1)}) custom-call(bf16[2,512,512]{2,1,0:T(8,128)(2,1)S(1)} %get-tuple-element.229.lhs_ref, bf16[2,512,512]{2,1,0:T(8,128)(2,1)S(1)} %get-tuple-element.230.forward_ref, bf16[512,4096]{1,0:T(8,128)(2,1)S(1)} %get-tuple-element.215.up_ref, ...), custom_call_target="tpu_custom_call" | custom-call | bytes 8388608 | tf_op jit(solution)/shard_map/cond/branch_0_fun/pallas_call | solution.py:464
  68.8 0.7 collective-permute-start.11
  69.5 7.3 %collective-permute-start.8 = (bf16[48,4096]{1,0:T(8,128)(2,1)S(1)}, bf16[48,4096]{1,0:T(8,128)(2,1)S(1)}, u32[]{:S(2)}, u32[]{:S(2)}) collective-permute-start(bf16[48,4096]{1,0:T(8,128)(2,1)S(1)} %get-tuple-element.236), channel_id=1, source_target_pairs={{0,4},{4,0},{8,12},{12,8},{1,5},{5,1},{9,13},{13,9},{2,6},{6,2},{1... | collective-permute-start | bytes 1179656 | tf_op jit(solution)/shard_map/cond/branch_0_fun/ppermute | solution.py:560
  76.8 1.6 %collective-permute-start.1 = (bf16[64,4096]{1,0:T(8,128)(2,1)S(1)}, bf16[64,4096]{1,0:T(8,128)(2,1)S(1)}, u32[]{:S(2)}, u32[]{:S(2)}) collective-permute-start(bf16[64,4096]{1,0:T(8,128)(2,1)S(1)} %branch_0_fun.12.mine_ref), channel_id=1, source_target_pairs={{0,16},{16,0},{1,17},{17,1},{2,18},{18,2},{3,19},{19,3},{4,20},{20... | collective-permute-start | bytes 1572872 | tf_op jit(solution)/shard_map/cond/branch_0_fun/ppermute | solution.py:567
  78.4 2.1 %branch_0_fun.18 = (bf16[48,4096]{1,0:T(8,128)(2,1)S(1)}, bf16[48,4096]{1,0:T(8,128)(2,1)S(1)}) custom-call(bf16[2,512,512]{2,1,0:T(8,128)(2,1)S(1)} %get-tuple-element.229.lhs_ref, bf16[2,512,512]{2,1,0:T(8,128)(2,1)S(1)} %get-tuple-element.230.forward_ref, bf16[512,4096]{1,0:T(8,128)(2,1)S(1)} %get-tuple-element.215.up_ref, ...), custom_call_target="tpu_custom_call" | custom-call | bytes 9437184 | tf_op jit(solution)/shard_map/cond/branch_0_fun/pallas_call | solution.py:464
  80.6 0.7 collective-permute-start.10
  82.0 4.8 %collective-permute-done.8.refs_4_ = bf16[48,4096]{1,0:T(8,128)(2,1)S(1)} collective-permute-done((bf16[48,4096]{1,0:T(8,128)(2,1)S(1)}, bf16[48,4096]{1,0:T(8,128)(2,1)S(1)}, u32[]{:S(2)}, u32[]{:S(2)}) %collective-permute-start.8) | collective-permute-done | bytes 393248 | tf_op jit(solution)/shard_map/cond/branch_0_fun/ppermute | solution.py:560
  86.8 2.3 %branch_0_fun.20 = (bf16[32,4096]{1,0:T(8,128)(2,1)S(1)}, bf16[32,4096]{1,0:T(8,128)(2,1)S(1)}) custom-call(bf16[2,512,512]{2,1,0:T(8,128)(2,1)S(1)} %get-tuple-element.229.lhs_ref, bf16[2,512,512]{2,1,0:T(8,128)(2,1)S(1)} %get-tuple-element.230.forward_ref, bf16[512,4096]{1,0:T(8,128)(2,1)S(1)} %get-tuple-element.215.up_ref, ...), custom_call_target="tpu_custom_call" | custom-call | bytes 10485760 | tf_op jit(solution)/shard_map/cond/branch_0_fun/pallas_call | solution.py:464
  89.1 2.1 %collective-permute-start.13 = (bf16[32,4096]{1,0:T(8,128)(2,1)S(1)}, bf16[32,4096]{1,0:T(8,128)(2,1)S(1)}, u32[]{:S(2)}, u32[]{:S(2)}) collective-permute-start(bf16[32,4096]{1,0:T(8,128)(2,1)S(1)} %get-tuple-element.241), channel_id=1, source_target_pairs={{0,4},{4,0},{8,12},{12,8},{1,5},{5,1},{9,13},{13,9},{2,6},{6,2},{1... | collective-permute-start | bytes 786440 | tf_op jit(solution)/shard_map/cond/branch_0_fun/ppermute | solution.py:560
  91.8 3.4 %collective-permute-done.10.refs_5_ = bf16[48,4096]{1,0:T(8,128)(2,1)S(1)} collective-permute-done((bf16[48,4096]{1,0:T(8,128)(2,1)S(1)}, bf16[48,4096]{1,0:T(8,128)(2,1)S(1)}, u32[]{:S(2)}, u32[]{:S(2)}) %collective-permute-start.10) | collective-permute-done | bytes 393248 | tf_op jit(solution)/shard_map/cond/branch_0_fun/ppermute | solution.py:560
  95.2 4.6 %branch_0_fun.19.early_ref = bf16[2,128,4096]{2,1,0:T(8,128)(2,1)S(1)} custom-call(bf16[2,256,512]{2,1,0:T(8,128)(2,1)S(1)} %get-tuple-element.202.arrive_ref, bf16[256,512]{1,0:T(8,128)(2,1)S(1)} %get-tuple-element.227.local_ref, bf16[512,4096]{1,0:T(8,128)(2,1)S(1)} %get-tuple-element.215.up_ref, bf16[48,4096]{1,0:T(8,128)(2,1)S(1)} %collective-permute-done.2.refs_0_, ...), custom_call_target="tpu_custom_call" | custom-call | bytes 1048576 | tf_op jit(solution)/shard_map/cond/branch_0_fun/pallas_call | solution.py:464
  99.9 2.9 %branch_0_fun.21 = bf16[64,2,4096]{2,1,0:T(2,128)(2,1)S(1)} custom-call(s32[1]{0:T(128)} %bitcast.group_ref, bf16[2,256,512]{2,1,0:T(8,128)(2,1)S(1)} %get-tuple-element.202.arrive_ref, bf16[128,64]{1,0:T(8,128)(2,1)S(1)} %get-tuple-element.204.panel_ref, bf16[64,4096]{1,0:T(8,128)(2,1)S(1)} %branch_0_fun.12.mine_ref, ...), custom_call_target="tpu_custom_call" | custom-call | bytes 1048576 | tf_op jit(solution)/shard_map/cond/branch_0_fun/pallas_call | solution.py:464
  103.3 1.0 copy-done.6
  104.3 0.9 copy-done.1
  (44 shorter events, 3.3 us)
Async XLA Ops:
  0.0 1.5 %copy-start = (bf16[16,2,4096]{2,1,0:T(2,128)(2,1)S(1)}, bf16[16,2,4096]{2,1,0:T(2,128)(2,1)}, u32[]{:S(2)}) copy-start(bf16[16,2,4096]{2,1,0:T(2,128)(2,1)} %param.16) | copy-start | bytes 786436
  0.0 5.0 %collective-permute-start.89 = (s32[2,32,2]{1,2,0:T(2,128)}, s32[2,32,2]{1,2,0:T(2,128)S(1)}, u32[]{:S(2)}, u32[]{:S(2)}) collective-permute-start(s32[2,32,2]{1,2,0:T(2,128)} %param.13), channel_id=1, source_target_pairs={{0,0},{1,5},{2,10},{3,15},{4,4},{5,9},{6,14},{7,3},{8,8},{9,13},{1... | collective-permute-start | bytes 1544 | tf_op jit(solution)/shard_map/ppermute | solution.py:611
  1.9 23.8 %collective-permute-start.96 = (bf16[16,4096]{1,0:T(8,128)(2,1)S(1)}, bf16[16,4096]{1,0:T(8,128)(2,1)S(1)}, u32[]{:S(2)}, u32[]{:S(2)}) collective-permute-start(bf16[16,4096]{1,0:T(8,128)(2,1)S(1)} %bitcast.35), channel_id=1, source_target_pairs={{0,4},{4,0},{8,12},{12,8},{1,5},{5,1},{9,13},{13,9},{2,6},{6,2},{1... | collective-permute-start | bytes 393224 | tf_op jit(solution)/shard_map/ppermute | solution.py:477
  5.0 20.7 %collective-permute-start.93 = (bf16[64,1536]{1,0:T(8,128)(2,1)}, bf16[64,1536]{1,0:T(8,128)(2,1)S(1)}, u32[]{:S(2)}, u32[]{:S(2)}) collective-permute-start(bf16[64,1536]{1,0:T(8,128)(2,1)} %bitcast.26), channel_id=1, source_target_pairs={{0,4},{4,8},{8,12},{12,0},{1,5},{5,9},{9,13},{13,1},{2,6},{6,10},{... | collective-permute-start | bytes 589832 | tf_op jit(solution)/shard_map/ppermute | solution.py:605
  5.1 20.6 %collective-permute-start.94 = (bf16[64,1536]{1,0:T(8,128)(2,1)}, bf16[64,1536]{1,0:T(8,128)(2,1)S(1)}, u32[]{:S(2)}, u32[]{:S(2)}) collective-permute-start(bf16[64,1536]{1,0:T(8,128)(2,1)} %bitcast.27), channel_id=1, source_target_pairs={{0,8},{4,12},{8,0},{12,4},{1,9},{5,13},{9,1},{13,5},{2,10},{6,14},... | collective-permute-start | bytes 589832 | tf_op jit(solution)/shard_map/ppermute | solution.py:605
  8.1 17.7 %collective-permute-start.95 = (bf16[64,1536]{1,0:T(8,128)(2,1)}, bf16[64,1536]{1,0:T(8,128)(2,1)S(1)}, u32[]{:S(2)}, u32[]{:S(2)}) collective-permute-start(bf16[64,1536]{1,0:T(8,128)(2,1)} %bitcast.28), channel_id=1, source_target_pairs={{0,12},{4,0},{8,4},{12,8},{1,13},{5,1},{9,5},{13,9},{2,14},{6,2},{... | collective-permute-start | bytes 589832 | tf_op jit(solution)/shard_map/ppermute | solution.py:605
  10.7 1.5 %collective-permute-start.90 = (bf16[16,128]{1,0:T(8,128)(2,1)S(1)}, bf16[16,128]{1,0:T(8,128)(2,1)S(1)}, u32[]{:S(2)}, u32[]{:S(2)}) collective-permute-start(bf16[16,128]{1,0:T(8,128)(2,1)S(1)} %fusion.2.refs_0_), channel_id=1, source_target_pairs={{0,1},{1,0},{2,3},{3,2},{4,5},{5,4},{6,7},{7,6},{8,9},{9,8},{10,11... | collective-permute-start | bytes 12296 | tf_op jit(solution)/shard_map/ppermute | solution.py:616
  12.2 6.0 %collective-permute-start.91 = (bf16[32,128]{1,0:T(8,128)(2,1)S(1)}, bf16[32,128]{1,0:T(8,128)(2,1)S(1)}, u32[]{:S(2)}, u32[]{:S(2)}) collective-permute-start(bf16[32,128]{1,0:T(8,128)(2,1)S(1)} %pad_maximum_fusion), channel_id=1, source_target_pairs={{0,2},{2,0},{1,3},{3,1},{4,6},{6,4},{5,7},{7,5},{8,10},{10,8},{9,1... | collective-permute-start | bytes 24584 | tf_op jit(solution)/shard_map/ppermute | solution.py:617
  19.4 5.6 %collective-permute-start.92 = (f32[8,128]{1,0:T(8,128)S(1)}, f32[8,128]{1,0:T(8,128)S(1)}, u32[]{:S(2)}, u32[]{:S(2)}) collective-permute-start(f32[8,128]{1,0:T(8,128)S(1)} %get-tuple-element.474.own_ref), channel_id=1, source_target_pairs={{0,16},{16,0},{1,17},{17,1},{2,18},{18,2},{3,19},{19,3},{4,20},{20... | collective-permute-start | bytes 12296 | tf_op jit(solution)/shard_map/ppermute | solution.py:505
  21.0 2.2 %copy-start.2 = (bf16[16,2,16,4096]{3,2,1,0:T(8,128)(2,1)S(1)}, bf16[16,2,16,4096]{3,2,1,0:T(8,128)(2,1)}, u32[]{:S(2)}) copy-start(bf16[16,2,16,4096]{3,2,1,0:T(8,128)(2,1)} %param.15) | copy-start | bytes 12582916
  23.2 1.4 %copy-start.3 = (bf16[16,2,16,1536]{3,2,1,0:T(8,128)(2,1)S(1)}, bf16[16,2,16,1536]{3,2,1,0:T(8,128)(2,1)}, u32[]{:S(2)}) copy-start(bf16[16,2,16,1536]{3,2,1,0:T(8,128)(2,1)} %down_ref) | copy-start | bytes 4718596
  24.6 1.1 %copy-start.4 = (bf16[2,32,1536]{2,1,0:T(8,128)(2,1)S(1)}, bf16[2,32,1536]{2,1,0:T(8,128)(2,1)}, u32[]{:S(2)}) copy-start(bf16[2,32,1536]{2,1,0:T(8,128)(2,1)} %param.11) | copy-start | bytes 589828
  26.5 8.5 %collective-permute-start.100 = (bf16[32,4096]{1,0:T(8,128)(2,1)S(1)}, bf16[32,4096]{1,0:T(8,128)(2,1)S(1)}, u32[]{:S(2)}, u32[]{:S(2)}) collective-permute-start(bf16[32,4096]{1,0:T(8,128)(2,1)S(1)} %get-tuple-element.488), channel_id=1, source_target_pairs={{4,8},{8,4},{5,9},{9,5},{6,10},{10,6},{7,11},{11,7},{20,24},{24,20... | collective-permute-start | bytes 786440 | tf_op jit(solution)/shard_map/ppermute | solution.py:519
  27.2 2.8 %collective-permute-start.97 = (f32[32,512]{1,0:T(8,128)S(1)}, f32[32,512]{1,0:T(8,128)S(1)}, u32[]{:S(2)}, u32[]{:S(2)}) collective-permute-start(f32[32,512]{1,0:T(8,128)S(1)} %get-tuple-element.486.own_ref), channel_id=1, source_target_pairs={{0,1},{1,0},{2,3},{3,2},{4,5},{5,4},{6,7},{7,6},{8,9},{9,8},{10,11... | collective-permute-start | bytes 196616 | tf_op jit(solution)/shard_map/ppermute | solution.py:518
  27.2 4.8 %collective-permute-start.98 = (f32[32,512]{1,0:T(8,128)S(1)}, f32[32,512]{1,0:T(8,128)S(1)}, u32[]{:S(2)}, u32[]{:S(2)}) collective-permute-start(f32[32,512]{1,0:T(8,128)S(1)} %get-tuple-element.486.own_ref), channel_id=1, source_target_pairs={{0,2},{1,3},{2,0},{3,1},{4,6},{5,7},{6,4},{7,5},{8,10},{9,11},{10,... | collective-permute-start | bytes 196616 | tf_op jit(solution)/shard_map/ppermute | solution.py:518
  29.3 4.0 %collective-permute-start.99 = (f32[32,512]{1,0:T(8,128)S(1)}, f32[32,512]{1,0:T(8,128)S(1)}, u32[]{:S(2)}, u32[]{:S(2)}) collective-permute-start(f32[32,512]{1,0:T(8,128)S(1)} %get-tuple-element.486.own_ref), channel_id=1, source_target_pairs={{0,3},{1,2},{2,1},{3,0},{4,7},{5,6},{6,5},{7,4},{8,11},{9,10},{10,... | collective-permute-start | bytes 196616 | tf_op jit(solution)/shard_map/ppermute | solution.py:518
  33.4 1.6 %copy-start.5 = (bf16[2,32,2,2,4096]{4,3,2,1,0:T(2,128)(2,1)S(1)}, bf16[2,32,2,2,4096]{4,3,2,1,0:T(2,128)(2,1)}, u32[]{:S(2)}) copy-start(bf16[2,32,2,2,4096]{4,3,2,1,0:T(2,128)(2,1)} %param.12) | copy-start | bytes 6291460
  35.0 16.6 %collective-permute-start.2 = (bf16[48,4096]{1,0:T(8,128)(2,1)S(1)}, bf16[48,4096]{1,0:T(8,128)(2,1)S(1)}, u32[]{:S(2)}, u32[]{:S(2)}) collective-permute-start(bf16[48,4096]{1,0:T(8,128)(2,1)S(1)} %get-tuple-element.228), channel_id=1, source_target_pairs={{0,4},{4,0},{8,12},{12,8},{1,5},{5,1},{9,13},{13,9},{2,6},{6,2},{1... | collective-permute-start | bytes 1179656 | tf_op jit(solution)/shard_map/cond/branch_0_fun/ppermute | solution.py:560
  40.0 11.6 %collective-permute-start.3 = (bf16[48,4096]{1,0:T(8,128)(2,1)S(1)}, bf16[48,4096]{1,0:T(8,128)(2,1)S(1)}, u32[]{:S(2)}, u32[]{:S(2)}) collective-permute-start(bf16[48,4096]{1,0:T(8,128)(2,1)S(1)} %get-tuple-element.231), channel_id=1, source_target_pairs={{4,8},{8,4},{5,9},{9,5},{6,10},{10,6},{7,11},{11,7},{20,24},{24,20... | collective-permute-start | bytes 1179656 | tf_op jit(solution)/shard_map/cond/branch_0_fun/ppermute | solution.py:559
  42.2 16.1 %collective-permute-start = (bf16[48,4096]{1,0:T(8,128)(2,1)S(1)}, bf16[48,4096]{1,0:T(8,128)(2,1)S(1)}, u32[]{:S(2)}, u32[]{:S(2)}) collective-permute-start(bf16[48,4096]{1,0:T(8,128)(2,1)S(1)} %get-tuple-element.216), channel_id=1, source_target_pairs={{0,4},{4,0},{8,12},{12,8},{1,5},{5,1},{9,13},{13,9},{2,6},{6,2},{1... | collective-permute-start | bytes 1179656 | tf_op jit(solution)/shard_map/cond/branch_0_fun/ppermute | solution.py:560
  45.6 12.7 %collective-permute-start.5 = (bf16[48,4096]{1,0:T(8,128)(2,1)S(1)}, bf16[48,4096]{1,0:T(8,128)(2,1)S(1)}, u32[]{:S(2)}, u32[]{:S(2)}) collective-permute-start(bf16[48,4096]{1,0:T(8,128)(2,1)S(1)} %get-tuple-element.233), channel_id=1, source_target_pairs={{4,8},{8,4},{5,9},{9,5},{6,10},{10,6},{7,11},{11,7},{20,24},{24,20... | collective-permute-start | bytes 1179656 | tf_op jit(solution)/shard_map/cond/branch_0_fun/ppermute | solution.py:559
  53.6 13.1 %collective-permute-start.4 = (bf16[48,4096]{1,0:T(8,128)(2,1)S(1)}, bf16[48,4096]{1,0:T(8,128)(2,1)S(1)}, u32[]{:S(2)}, u32[]{:S(2)}) collective-permute-start(bf16[48,4096]{1,0:T(8,128)(2,1)S(1)} %get-tuple-element.232), channel_id=1, source_target_pairs={{0,4},{4,0},{8,12},{12,8},{1,5},{5,1},{9,13},{13,9},{2,6},{6,2},{1... | collective-permute-start | bytes 1179656 | tf_op jit(solution)/shard_map/cond/branch_0_fun/ppermute | solution.py:560
  55.9 10.8 %collective-permute-start.7 = (bf16[48,4096]{1,0:T(8,128)(2,1)S(1)}, bf16[48,4096]{1,0:T(8,128)(2,1)S(1)}, u32[]{:S(2)}, u32[]{:S(2)}) collective-permute-start(bf16[48,4096]{1,0:T(8,128)(2,1)S(1)} %get-tuple-element.235), channel_id=1, source_target_pairs={{4,8},{8,4},{5,9},{9,5},{6,10},{10,6},{7,11},{11,7},{20,24},{24,20... | collective-permute-start | bytes 1179656 | tf_op jit(solution)/shard_map/cond/branch_0_fun/ppermute | solution.py:559
  60.3 18.1 %collective-permute-start.6 = (bf16[48,4096]{1,0:T(8,128)(2,1)S(1)}, bf16[48,4096]{1,0:T(8,128)(2,1)S(1)}, u32[]{:S(2)}, u32[]{:S(2)}) collective-permute-start(bf16[48,4096]{1,0:T(8,128)(2,1)S(1)} %get-tuple-element.234), channel_id=1, source_target_pairs={{0,4},{4,0},{8,12},{12,8},{1,5},{5,1},{9,13},{13,9},{2,6},{6,2},{1... | collective-permute-start | bytes 1179656 | tf_op jit(solution)/shard_map/cond/branch_0_fun/ppermute | solution.py:560
  64.3 14.1 %collective-permute-start.9 = (bf16[48,4096]{1,0:T(8,128)(2,1)S(1)}, bf16[48,4096]{1,0:T(8,128)(2,1)S(1)}, u32[]{:S(2)}, u32[]{:S(2)}) collective-permute-start(bf16[48,4096]{1,0:T(8,128)(2,1)S(1)} %get-tuple-element.237), channel_id=1, source_target_pairs={{4,8},{8,4},{5,9},{9,5},{6,10},{10,6},{7,11},{11,7},{20,24},{24,20... | collective-permute-start | bytes 1179656 | tf_op jit(solution)/shard_map/cond/branch_0_fun/ppermute | solution.py:559
  68.8 13.2 %collective-permute-start.11 = (bf16[48,4096]{1,0:T(8,128)(2,1)S(1)}, bf16[48,4096]{1,0:T(8,128)(2,1)S(1)}, u32[]{:S(2)}, u32[]{:S(2)}) collective-permute-start(bf16[48,4096]{1,0:T(8,128)(2,1)S(1)} %get-tuple-element.239), channel_id=1, source_target_pairs={{4,8},{8,4},{5,9},{9,5},{6,10},{10,6},{7,11},{11,7},{20,24},{24,20... | collective-permute-start | bytes 1179656 | tf_op jit(solution)/shard_map/cond/branch_0_fun/ppermute | solution.py:559
  69.5 17.3 %collective-permute-start.8 = (bf16[48,4096]{1,0:T(8,128)(2,1)S(1)}, bf16[48,4096]{1,0:T(8,128)(2,1)S(1)}, u32[]{:S(2)}, u32[]{:S(2)}) collective-permute-start(bf16[48,4096]{1,0:T(8,128)(2,1)S(1)} %get-tuple-element.236), channel_id=1, source_target_pairs={{0,4},{4,0},{8,12},{12,8},{1,5},{5,1},{9,13},{13,9},{2,6},{6,2},{1... | collective-permute-start | bytes 1179656 | tf_op jit(solution)/shard_map/cond/branch_0_fun/ppermute | solution.py:560
  76.8 23.1 %collective-permute-start.1 = (bf16[64,4096]{1,0:T(8,128)(2,1)S(1)}, bf16[64,4096]{1,0:T(8,128)(2,1)S(1)}, u32[]{:S(2)}, u32[]{:S(2)}) collective-permute-start(bf16[64,4096]{1,0:T(8,128)(2,1)S(1)} %branch_0_fun.12.mine_ref), channel_id=1, source_target_pairs={{0,16},{16,0},{1,17},{17,1},{2,18},{18,2},{3,19},{19,3},{4,20},{20... | collective-permute-start | bytes 1572872 | tf_op jit(solution)/shard_map/cond/branch_0_fun/ppermute | solution.py:567
  80.6 14.7 %collective-permute-start.10 = (bf16[48,4096]{1,0:T(8,128)(2,1)S(1)}, bf16[48,4096]{1,0:T(8,128)(2,1)S(1)}, u32[]{:S(2)}, u32[]{:S(2)}) collective-permute-start(bf16[48,4096]{1,0:T(8,128)(2,1)S(1)} %get-tuple-element.238), channel_id=1, source_target_pairs={{0,4},{4,0},{8,12},{12,8},{1,5},{5,1},{9,13},{13,9},{2,6},{6,2},{1... | collective-permute-start | bytes 1179656 | tf_op jit(solution)/shard_map/cond/branch_0_fun/ppermute | solution.py:560
  81.3 13.9 %collective-permute-start.12 = (bf16[48,4096]{1,0:T(8,128)(2,1)S(1)}, bf16[48,4096]{1,0:T(8,128)(2,1)S(1)}, u32[]{:S(2)}, u32[]{:S(2)}) collective-permute-start(bf16[48,4096]{1,0:T(8,128)(2,1)S(1)} %get-tuple-element.240), channel_id=1, source_target_pairs={{4,8},{8,4},{5,9},{9,5},{6,10},{10,6},{7,11},{11,7},{20,24},{24,20... | collective-permute-start | bytes 1179656 | tf_op jit(solution)/shard_map/cond/branch_0_fun/ppermute | solution.py:559
  89.1 10.8 %collective-permute-start.13 = (bf16[32,4096]{1,0:T(8,128)(2,1)S(1)}, bf16[32,4096]{1,0:T(8,128)(2,1)S(1)}, u32[]{:S(2)}, u32[]{:S(2)}) collective-permute-start(bf16[32,4096]{1,0:T(8,128)(2,1)S(1)} %get-tuple-element.241), channel_id=1, source_target_pairs={{0,4},{4,0},{8,12},{12,8},{1,5},{5,1},{9,13},{13,9},{2,6},{6,2},{1... | collective-permute-start | bytes 786440 | tf_op jit(solution)/shard_map/cond/branch_0_fun/ppermute | solution.py:560
  91.2 8.7 %collective-permute-start.14 = (bf16[32,4096]{1,0:T(8,128)(2,1)S(1)}, bf16[32,4096]{1,0:T(8,128)(2,1)S(1)}, u32[]{:S(2)}, u32[]{:S(2)}) collective-permute-start(bf16[32,4096]{1,0:T(8,128)(2,1)S(1)} %get-tuple-element.242), channel_id=1, source_target_pairs={{4,8},{8,4},{5,9},{9,5},{6,10},{10,6},{7,11},{11,7},{20,24},{24,20... | collective-permute-start | bytes 786440 | tf_op jit(solution)/shard_map/cond/branch_0_fun/ppermute | solution.py:559
  103.3 1.0 copy-start.6
  104.3 0.9 copy-start.1
